TPU v7x, 512 devices: a whole 4x4x16 slice. The times are simulated.
512 devices in a mesh: dp: 4 (over x), ctx: 16 (over z), head: 8 (over y, core).
Axes of the slice: x: 4, y: 4, z: 16, core: 2. Of those that a mesh axis runs over, the one named last changes fastest.
Arguments:
- queries: bfloat16 [8192, 4096], P(('dp', 'ctx'), 'head'), parts along dimension 0, may hold values from -4.5 to 4.5
- context_keys: bfloat16 [131072, 1024], P(('dp', 'ctx'), 'head'), parts along dimension 0, may hold values from -4.5 to 4.5
- context_values: bfloat16 [131072, 1024], P(('dp', 'ctx'), 'head'), parts along dimension 0, may hold values from -4.5 to 4.5
- own_keys: bfloat16 [8192, 1024], P(('dp', 'ctx'), 'head'), parts along dimension 0, may hold values from -4.5 to 4.5
- own_values: bfloat16 [8192, 1024], P(('dp', 'ctx'), 'head'), parts along dimension 0, may hold values from -4.5 to 4.5
- out_grad: bfloat16 [8192, 4096], P(('dp', 'ctx'), 'head'), parts along dimension 0, may hold values from -4.5 to 4.5
- block_ids: int32 [64, 24], P('dp'), parts along dimension 0, may hold values from -1 to 255, as said below
Outputs:
- attended: bfloat16 [8192, 4096], P(('dp', 'ctx'), 'head'), parts along dimension 0
- query_grad: bfloat16 [8192, 4096], P(('dp', 'ctx'), 'head'), parts along dimension 0
- key_grad: bfloat16 [131072, 1024], P(('dp', 'ctx'), 'head'), parts along dimension 0
- value_grad: bfloat16 [131072, 1024], P(('dp', 'ctx'), 'head'), parts along dimension 0
- own_key_grad: bfloat16 [8192, 1024], P(('dp', 'ctx'), 'head'), parts along dimension 0
- own_value_grad: bfloat16 [8192, 1024], P(('dp', 'ctx'), 'head'), parts along dimension 0
There are 4 independent parts, one for each index of `dp`. A program takes and returns all parts, laid end to end along the dimension named above; each array names one. Nothing has to cross between parts.
Inputs may be any that keep to these rules, and one draw needn't show every extreme that they name: `block_ids`: each row lists distinct blocks in ascending order, then -1 in unused slots. At most 2 listed blocks of one row have the same b // 16, and some row reaches that; some row fills all 24 slots.
All inputs are finite; a program needn't handle non-finite values.
Results may differ from a plain program's by a relative error of at most 0.012.
The roundings to bfloat16 on the way count: a program that leaves them out, or rounds other values in their place, can miss the bound.
Values may be sent and summed in bfloat16 or wider, within the bound.
A program may use at most 128 MiB of HBM per device.

v0:
```python
import math

import jax
import jax.numpy as jnp
from jax import lax
from jax.sharding import PartitionSpec as P

QH = 32
KVH = 8
DH = 128
BLK = 128
CLEN = 128
PER_SRC = 2


MASKED_SCORE = -1e30


def score_rows(query_rows, key_rows, visible):
    scores = jnp.einsum(
        "bigrd,bjgd->bgrij", query_rows, key_rows, preferred_element_type=jnp.float32
    )
    scores = scores * (1.0 / math.sqrt(query_rows.shape[-1]))
    return jnp.where(visible, scores, MASKED_SCORE)


def partial_stats(scores, visible):
    maxima = jnp.max(scores, axis=-1)
    totals = jnp.sum(jnp.where(visible, jnp.exp(scores - maxima[..., None]), 0.0), axis=-1)
    return (maxima, totals)


def soft_weights(scores, visible, logsum):
    weights = jnp.where(visible, jnp.exp(scores - logsum[..., None]), 0.0)
    return (weights, weights.astype(jnp.bfloat16))


def weighted_values(rounded, value_rows):
    return jnp.einsum("bgrij,bjgd->bigrd", rounded, value_rows, preferred_element_type=jnp.float32)


def local_weighted(scores, visible, maxima, value_rows):
    local = jnp.where(visible, jnp.exp(scores - maxima[..., None]), 0.0).astype(jnp.bfloat16)
    return weighted_values(local, value_rows)


def rescale(partial_value, maxima, logsum):
    return partial_value * jnp.exp(maxima - logsum).transpose(0, 3, 1, 2)[..., None]


def combine_stats(own_max, own_total, back_max, back_total):
    top_max = jnp.maximum(own_max[0], jnp.max(back_max, axis=0))
    top_total = own_total[0] * jnp.exp(own_max[0] - top_max) + jnp.sum(
        back_total * jnp.exp(back_max - top_max[None]), axis=0
    )
    return (top_max + jnp.log(top_total))[None]


def row_deltas(grad_rows, output):
    return jnp.sum(grad_rows.astype(jnp.float32) * output, axis=-1).transpose(0, 2, 3, 1)


def gradient_terms(query_rows, key_rows, value_rows, grad_rows, weights, rounded, deltas):
    score_scale = 1.0 / math.sqrt(query_rows.shape[-1])
    grad_weights = jnp.einsum(
        "bigrd,bjgd->bgrij", grad_rows, value_rows, preferred_element_type=jnp.float32
    )
    grad_scores = (weights * (grad_weights - deltas[..., None])).astype(jnp.bfloat16)
    query_grad = (
        jnp.einsum("bgrij,bjgd->bigrd", grad_scores, key_rows, preferred_element_type=jnp.float32)
        * score_scale
    )
    key_grad = (
        jnp.einsum("bgrij,bigrd->bjgd", grad_scores, query_rows, preferred_element_type=jnp.float32)
        * score_scale
    )
    value_grad = jnp.einsum(
        "bgrij,bigrd->bjgd", rounded, grad_rows, preferred_element_type=jnp.float32
    )
    return (query_grad, key_grad, value_grad)


def block_sums(zero_sums, flat_index, flat_live, grads):
    rows = grads.reshape(flat_index.shape[0], zero_sums.shape[1], zero_sums.shape[2])
    return zero_sums.at[flat_index].add(jnp.where(flat_live, rows, 0.0))


def far_setup(
    every_query,
    every_grad,
    key_blocks,
    value_blocks,
    local_index,
    slot_live,
    peer_count,
    groups,
    group_ratio,
):
    all_queries = every_query.reshape(peer_count, CLEN, groups, group_ratio, DH)
    all_grads = every_grad.reshape(peer_count, CLEN, groups, group_ratio, DH)
    near_keys = key_blocks[local_index].reshape(peer_count, PER_SRC * BLK, groups, DH)
    near_values = value_blocks[local_index].reshape(peer_count, PER_SRC * BLK, groups, DH)
    far_visible = jnp.repeat(slot_live, BLK, axis=1)[:, None, None, None, :]
    far_scores = score_rows(all_queries, near_keys, far_visible)
    return (all_queries, all_grads, near_keys, near_values, far_visible, far_scores)


def on_device(queries, context_keys, context_values, own_keys, own_values, out_grad, block_ids):
    peer_count = lax.axis_size("ctx")
    my_index = lax.axis_index("ctx")
    groups = context_keys.shape[1] // DH
    group_ratio = QH // KVH
    block_count = context_keys.shape[0] // BLK
    list_width = block_ids.shape[1]
    query_rows = queries.reshape(1, CLEN, groups, group_ratio, DH)
    grad_rows = out_grad.reshape(1, CLEN, groups, group_ratio, DH)
    own_key_rows = own_keys.reshape(1, CLEN, groups, DH)
    own_value_rows = own_values.reshape(1, CLEN, groups, DH)
    key_blocks = context_keys.reshape(block_count, BLK, groups * DH)
    value_blocks = context_values.reshape(block_count, BLK, groups * DH)
    listed_live = block_ids >= 0
    block_low = my_index * block_count
    in_range = listed_live & (block_ids >= block_low) & (block_ids < block_low + block_count)
    first_pos = jnp.sum(listed_live & (block_ids < block_low), axis=1, dtype=jnp.int32)
    slot_count = jnp.sum(in_range, axis=1, dtype=jnp.int32)
    slot_rank = jnp.arange(PER_SRC, dtype=jnp.int32)
    slot_pos = jnp.minimum(first_pos[:, None] + slot_rank[None, :], list_width - 1)
    picked = jnp.take_along_axis(block_ids, slot_pos, axis=1) - block_low
    slot_live = slot_rank[None, :] < slot_count[:, None]
    local_index = jnp.where(slot_live, picked, 0)
    flat_index = local_index.reshape(-1)
    flat_live = slot_live.reshape(-1)[:, None, None]
    causal = jnp.arange(CLEN)[:, None] >= jnp.arange(CLEN)[None, :]
    zero_sums = jnp.zeros((block_count, BLK, groups * DH), jnp.float32)
    own_visible = causal[None, None, None]
    every_query, every_grad = (
        lax.all_gather(queries, "ctx", axis=0, tiled=True),
        lax.all_gather(out_grad, "ctx", axis=0, tiled=True),
    )
    all_queries, all_grads, near_keys, near_values, far_visible, far_scores = far_setup(
        every_query,
        every_grad,
        key_blocks,
        value_blocks,
        local_index,
        slot_live,
        peer_count,
        groups,
        group_ratio,
    )
    far_max, far_total = partial_stats(far_scores, far_visible)
    back_max, back_total = (
        lax.all_to_all(far_max, "ctx", split_axis=0, concat_axis=0, tiled=True),
        lax.all_to_all(far_total, "ctx", split_axis=0, concat_axis=0, tiled=True),
    )
    own_scores = score_rows(query_rows, own_key_rows, own_visible)
    own_max, own_total = partial_stats(own_scores, own_visible)
    logsum = combine_stats(own_max, own_total, back_max, back_total)
    every_logsum = lax.all_gather(logsum, "ctx", axis=0, tiled=True)
    far_output = rescale(
        local_weighted(far_scores, far_visible, far_max, near_values), far_max, every_logsum
    )
    back_output = lax.all_to_all(far_output, "ctx", split_axis=0, concat_axis=0, tiled=True)
    own_weights, own_rounded = soft_weights(own_scores, own_visible, logsum)
    own_output = rescale(
        local_weighted(own_scores, own_visible, own_max, own_value_rows), own_max, logsum
    )
    output = own_output + jnp.sum(back_output, axis=0, keepdims=True)
    deltas = row_deltas(grad_rows, output)
    every_delta = lax.all_gather(deltas, "ctx", axis=0, tiled=True)
    far_weights, far_rounded = soft_weights(far_scores, far_visible, every_logsum)
    far_qgrad, far_kgrad, far_vgrad = gradient_terms(
        all_queries, near_keys, near_values, all_grads, far_weights, far_rounded, every_delta
    )
    back_qgrad = lax.all_to_all(far_qgrad, "ctx", split_axis=0, concat_axis=0, tiled=True)
    own_qgrad, own_kgrad, own_vgrad = gradient_terms(
        query_rows, own_key_rows, own_value_rows, grad_rows, own_weights, own_rounded, deltas
    )
    query_grad = own_qgrad + jnp.sum(back_qgrad, axis=0, keepdims=True)
    key_sums = block_sums(zero_sums, flat_index, flat_live, far_kgrad)
    value_sums = block_sums(zero_sums, flat_index, flat_live, far_vgrad)
    head_width = groups * group_ratio * DH
    attended = output.astype(jnp.bfloat16).reshape(CLEN, head_width)
    query_out = query_grad.astype(jnp.bfloat16).reshape(CLEN, head_width)
    key_out = key_sums.astype(jnp.bfloat16).reshape(block_count * BLK, groups * DH)
    value_out = value_sums.astype(jnp.bfloat16).reshape(block_count * BLK, groups * DH)
    own_key_out = own_kgrad.astype(jnp.bfloat16).reshape(CLEN, groups * DH)
    own_value_out = own_vgrad.astype(jnp.bfloat16).reshape(CLEN, groups * DH)
    return (attended, query_out, key_out, value_out, own_key_out, own_value_out)


def solution(mesh):
    placed = (
        P(("dp", "ctx"), "head"),
        P(("dp", "ctx"), "head"),
        P(("dp", "ctx"), "head"),
        P(("dp", "ctx"), "head"),
        P(("dp", "ctx"), "head"),
        P(("dp", "ctx"), "head"),
        P("dp", None),
    )
    return jax.shard_map(
        on_device,
        mesh=mesh,
        in_specs=placed,
        out_specs=(
            P(("dp", "ctx"), "head"),
            P(("dp", "ctx"), "head"),
            P(("dp", "ctx"), "head"),
            P(("dp", "ctx"), "head"),
            P(("dp", "ctx"), "head"),
            P(("dp", "ctx"), "head"),
        ),
        check_vma=False,
    )
```

profile of v0, /device:TPU:6, one launch (start us, length us, event | category | flops | bytes accessed | tf_op | source)
XLA Modules:
  0.0 599.3 jit_solution(13155322698787681609)
XLA Ops:
  12.4 75.2 %all-gather.3.cloned.1.call-done = bf16[2048,512]{1,0:T(8,128)(2,1)} async-done(((bf16[128,512]{1,0:T(8,128)(2,1)}), bf16[2048,512]{1,0:T(8,128)(2,1)}) %all-gather.3.cloned.1.call-update) | async-done | bytes 2097168 | tf_op jit(solution)/shard_map/all_gather | solution.py:137
  87.6 4.0 reshape.638
  91.6 6.0 bitcast_reduce_fusion
  97.5 7.9 %all-to-all-start = ((f32[16,1,4,128]{3,2,1,0:T(4,128)}), f32[16,1,4,128]{3,2,1,0:T(4,128)S(1)}, u32[]{:S(2)}, u32[]{:S(2)}) async-start(f32[16,1,4,128]{3,2,1,0:T(4,128)} %bitcast.15), calls=%async_computation | async-start | bytes 65536 | tf_op jit(solution)/shard_map/all_to_all | solution.py:153
  105.5 5.9 fusion.8
  111.4 6.7 %all-to-all-done = f32[16,1,4,128]{3,2,1,0:T(4,128)S(1)} async-done(((f32[16,1,4,128]{3,2,1,0:T(4,128)}), f32[16,1,4,128]{3,2,1,0:T(4,128)S(1)}, u32[]{:S(2)}, u32[]{:S(2)}) %all-to-all-start) | async-done | bytes 32800 | tf_op jit(solution)/shard_map/all_to_all | solution.py:153
  118.1 5.3 all-to-all-start.1
  123.5 12.5 %all-to-all-done.1 = f32[16,1,4,128]{3,2,1,0:T(4,128)S(1)} async-done(((f32[16,1,4,128]{3,2,1,0:T(4,128)}), f32[16,1,4,128]{3,2,1,0:T(4,128)S(1)}, u32[]{:S(2)}, u32[]{:S(2)}) %all-to-all-start.1) | async-done | bytes 32800 | tf_op jit(solution)/shard_map/all_to_all | solution.py:154
  136.7 30.1 %all_gather.13 = f32[16,1,4,128]{3,2,1,0:T(4,128)S(1)} all-gather(f32[1,1,4,128]{3,2,1,0:T(4,128)S(1)} %get-tuple-element.27), channel_id=1, replica_groups=mesh['dp'=4,'ctx'=16,'head'=8] {'ctx'}, dimensions={0}, use_global_device_ids=true | all-gather | bytes 34816 | tf_op jit(solution)/shard_map/all_gather | solution.py:159
  167.6 6.3 %fusion.14 = f32[16,128,1,4,128]{1,4,3,2,0:T(8,128)} fusion(f32[16,128,4]{1,2,0:T(4,128)S(1)} %exponential_bitcast_fusion, bf16[16,256,128,1]{2,1,3,0:T(8,128)(2,1)S(1)} %bitcast.329, f32[16,256,128,4]{2,1,3,0:T(8,128)} %get-tuple-element.35, f32[16,4,128]{2,1,0:T(4,128)} %get-tuple-element.34, pred[16,256]{1,0:T(8,128)(4,1)S(1)} %bitcast.340), kind=kOutput, calls=%fused_computation.24 | convolution fusion | flops 548405248 | bytes 13701120 | tf_op jit(solution)/shard_map/bgrij,bjgd->bigrd/dot_general | solution.py:39
  173.9 4.7 all-to-all-start.2
  180.2 149.1 %all-gather.5.cloned.1.call-done = bf16[2048,512]{1,0:T(8,128)(2,1)} async-done(((bf16[128,512]{1,0:T(8,128)(2,1)}), bf16[2048,512]{1,0:T(8,128)(2,1)}) %all-gather.5.cloned.1.call-update) | async-done | bytes 2097168 | tf_op jit(solution)/shard_map/all_gather | solution.py:138
  329.3 4.0 reshape.639
  333.3 28.2 %all-to-all-done.2 = f32[16,128,1,4,128]{1,4,3,2,0:T(8,128)} async-done(((f32[16,128,1,4,128]{1,4,3,2,0:T(8,128)}), f32[16,128,1,4,128]{1,4,3,2,0:T(8,128)}, u32[]{:S(2)}, u32[]{:S(2)}) %all-to-all-start.2) | async-done | bytes 4194336 | tf_op jit(solution)/shard_map/all_to_all | solution.py:163
  361.5 2.4 reduce_sum.88
  365.2 29.7 %all_gather.15 = f32[16,1,4,128]{3,2,1,0:T(4,128)S(1)} all-gather(f32[1,1,4,128]{3,2,1,0:T(4,128)S(1)} %bitcast.345), channel_id=1, replica_groups=mesh['dp'=4,'ctx'=16,'head'=8] {'ctx'}, dimensions={0}, use_global_device_ids=true | all-gather | bytes 34816 | tf_op jit(solution)/shard_map/all_gather | solution.py:170
  394.9 7.1 %fusion.13 = bf16[16,4,128,256]{2,3,1,0:T(8,128)(2,1)S(1)} fusion(f32[16,256,128,4]{2,1,3,0:T(8,128)} %get-tuple-element.35, f32[16,4,128]{2,1,0:T(4,128)S(1)} %bitcast.344, f32[16,4,128]{2,1,0:T(4,128)} %bitcast.336, pred[16,256]{1,0:T(8,128)(4,1)} %bitcast.341, bf16[16,256,128,1]{2,1,3,0:T(8,128)(2,1)S(1)} %bitcast.330, ...), kind=kOutput, calls=%fused_computation.22 | convolution fusion | flops 551550976 | bytes 15798272 | tf_op jit(solution)/shard_map/bigrd,bjgd->bgrij/dot_general | solution.py:65
  404.0 2.8 multiply_bitcast_fusion
  406.8 9.5 %all-to-all-start.3 = ((f32[16,128,1,4,128]{1,4,3,2,0:T(8,128)}), f32[16,128,1,4,128]{1,4,3,2,0:T(8,128)}, u32[]{:S(2)}, u32[]{:S(2)}) async-start(f32[16,128,1,4,128]{1,4,3,2,0:T(8,128)} %multiply_bitcast_fusion), calls=%async_computation.3 | async-start | bytes 8388608 | tf_op jit(solution)/shard_map/all_to_all | solution.py:175
  417.7 5.4 fusion.19
  424.8 2.7 broadcast_select_fusion
  427.7 4.7 scatter_fusion.1
  433.3 4.7 scatter_fusion
  440.7 148.3 %all-to-all-done.3 = f32[16,128,1,4,128]{1,4,3,2,0:T(8,128)} async-done(((f32[16,128,1,4,128]{1,4,3,2,0:T(8,128)}), f32[16,128,1,4,128]{1,4,3,2,0:T(8,128)}, u32[]{:S(2)}, u32[]{:S(2)}) %all-to-all-start.3) | async-done | bytes 4194336 | tf_op jit(solution)/shard_map/all_to_all | solution.py:175
  (109 shorter events, 21.5 us)
Async XLA Ops:
  7.2 80.4 %all-gather.3.cloned.1.call-start = ((), (), s32[]{:S(2)}) async-start(), calls=%async_computation.4 | async-start | bytes 2228224 | tf_op jit(solution)/shard_map/all_gather | solution.py:137
  10.1 157.5 %copy-start.17 = (pred[2,8,2,128]{3,1,2,0:T(8,128)(4,1)}, pred[2,8,2,128]{3,1,2,0:T(8,128)(4,1)S(1)}, u32[]{:S(2)}) copy-start(pred[2,8,2,128]{3,1,2,0:T(8,128)(4,1)S(1)} %copy.130) | copy-start | bytes 12292
  12.4 123.7 %copy-start.15 = (f32[4,128]{1,0:T(4,128)}, f32[4,128]{1,0:T(4,128)S(1)}, u32[]{:S(2)}) copy-start(f32[4,128]{1,0:T(4,128)S(1)} %get-tuple-element.32) | copy-start | bytes 6148
  97.5 20.6 %all-to-all-start = ((f32[16,1,4,128]{3,2,1,0:T(4,128)}), f32[16,1,4,128]{3,2,1,0:T(4,128)S(1)}, u32[]{:S(2)}, u32[]{:S(2)}) async-start(f32[16,1,4,128]{3,2,1,0:T(4,128)} %bitcast.15), calls=%async_computation | async-start | bytes 65536 | tf_op jit(solution)/shard_map/all_to_all | solution.py:153
  118.1 17.9 %all-to-all-start.1 = ((f32[16,1,4,128]{3,2,1,0:T(4,128)}), f32[16,1,4,128]{3,2,1,0:T(4,128)S(1)}, u32[]{:S(2)}, u32[]{:S(2)}) async-start(f32[16,1,4,128]{3,2,1,0:T(4,128)} %bitcast.18), calls=%async_computation.1 | async-start | bytes 65536 | tf_op jit(solution)/shard_map/all_to_all | solution.py:154
  123.5 13.2 %copy-start.23 = (f32[4,128]{1,0:T(4,128)}, f32[4,128]{1,0:T(4,128)S(1)}, u32[]{:S(2)}) copy-start(f32[4,128]{1,0:T(4,128)S(1)} %fusion.49) | copy-start | bytes 6148
  123.5 13.2 %copy-start.25 = (f32[4,128]{1,0:T(4,128)}, f32[4,128]{1,0:T(4,128)S(1)}, u32[]{:S(2)}) copy-start(f32[4,128]{1,0:T(4,128)S(1)} %max.28) | copy-start | bytes 6148
  173.9 187.6 %all-to-all-start.2 = ((f32[16,128,1,4,128]{1,4,3,2,0:T(8,128)}), f32[16,128,1,4,128]{1,4,3,2,0:T(8,128)}, u32[]{:S(2)}, u32[]{:S(2)}) async-start(f32[16,128,1,4,128]{1,4,3,2,0:T(8,128)} %fusion.14), calls=%async_computation.2 | async-start | bytes 8388608 | tf_op jit(solution)/shard_map/all_to_all | solution.py:163
  178.7 150.6 %all-gather.5.cloned.1.call-start = ((), (), s32[]{:S(2)}) async-start(), calls=%async_computation.5 | async-start | bytes 2228224 | tf_op jit(solution)/shard_map/all_gather | solution.py:138
  365.2 29.7 %copy-start.21 = (f32[128,4]{0,1:T(4,128)}, f32[128,4]{0,1:T(4,128)S(1)}, u32[]{:S(2)}) copy-start(f32[128,4]{0,1:T(4,128)S(1)} %get-tuple-element.28) | copy-start | bytes 6148
  406.7 9.6 %copy-start.20 = (pred[16,2]{1,0:T(8,128)(4,1)S(1)}, pred[16,2]{1,0:T(8,128)(4,1)}, u32[]{:S(2)}) copy-start(pred[16,2]{1,0:T(8,128)(4,1)} %copy-done.19) | copy-start | bytes 100
  406.7 9.8 %copy-start.30 = (s32[16]{0:T(128)S(1)}, s32[16]{0:T(128)}, u32[]{:S(2)}) copy-start(s32[16]{0:T(128)} %copy-done.29) | copy-start | bytes 196
  406.7 10.1 %copy-start.9 = (s32[32]{0:T(128)S(1)}, s32[32]{0:T(128)}, u32[]{:S(2)}) copy-start(s32[32]{0:T(128)} %copy-done.8) | copy-start | bytes 388
  406.7 10.1 %copy-start.16 = (f32[4,128]{1,0:T(4,128)S(1)}, f32[4,128]{1,0:T(4,128)}, u32[]{:S(2)}) copy-start(f32[4,128]{1,0:T(4,128)} %copy-done.15) | copy-start | bytes 6148
  406.8 10.1 %copy-start.24 = (f32[4,128]{1,0:T(4,128)S(1)}, f32[4,128]{1,0:T(4,128)}, u32[]{:S(2)}) copy-start(f32[4,128]{1,0:T(4,128)} %copy-done.23) | copy-start | bytes 6148
  406.8 10.1 %copy-start.26 = (f32[4,128]{1,0:T(4,128)S(1)}, f32[4,128]{1,0:T(4,128)}, u32[]{:S(2)}) copy-start(f32[4,128]{1,0:T(4,128)} %copy-done.25) | copy-start | bytes 6148
  406.8 10.1 %copy-start.28 = (f32[4,128]{1,0:T(4,128)S(1)}, f32[4,128]{1,0:T(4,128)}, u32[]{:S(2)}) copy-start(f32[4,128]{1,0:T(4,128)} %copy-done.27) | copy-start | bytes 6148
  406.8 10.9 %copy-start.13 = (f32[16,1,4,128]{3,2,1,0:T(4,128)S(1)}, f32[16,1,4,128]{3,2,1,0:T(4,128)}, u32[]{:S(2)}) copy-start(f32[16,1,4,128]{3,2,1,0:T(4,128)} %copy-done.12) | copy-start | bytes 98308
  406.8 10.9 %copy-start.18 = (pred[2,8,2,128]{3,1,2,0:T(8,128)(4,1)S(1)}, pred[2,8,2,128]{3,1,2,0:T(8,128)(4,1)}, u32[]{:S(2)}) copy-start(pred[2,8,2,128]{3,1,2,0:T(8,128)(4,1)} %copy-done.17) | copy-start | bytes 12292
  406.8 182.2 %all-to-all-start.3 = ((f32[16,128,1,4,128]{1,4,3,2,0:T(8,128)}), f32[16,128,1,4,128]{1,4,3,2,0:T(8,128)}, u32[]{:S(2)}, u32[]{:S(2)}) async-start(f32[16,128,1,4,128]{1,4,3,2,0:T(8,128)} %multiply_bitcast_fusion), calls=%async_computation.3 | async-start | bytes 8388608 | tf_op jit(solution)/shard_map/all_to_all | solution.py:175
  417.7 5.9 copy-start.4
  433.3 6.4 %copy-start.14 = (bf16[128,128]{1,0:T(8,128)(2,1)S(1)}, bf16[128,128]{1,0:T(8,128)(2,1)}, u32[]{:S(2)}) copy-start(bf16[128,128]{1,0:T(8,128)(2,1)} %param.11) | copy-start | bytes 98308
  433.3 6.4 %copy-start.22 = (f32[128,4]{0,1:T(4,128)S(1)}, f32[128,4]{0,1:T(4,128)}, u32[]{:S(2)}) copy-start(f32[128,4]{0,1:T(4,128)} %copy-done.21) | copy-start | bytes 6148
  438.0 153.4 %copy-start.11 = (bf16[128,128]{1,0:T(8,128)(2,1)S(1)}, bf16[128,128]{1,0:T(8,128)(2,1)}, u32[]{:S(2)}) copy-start(bf16[128,128]{1,0:T(8,128)(2,1)} %param.10) | copy-start | bytes 98308
  (13 other events, 29.0 us)
Sparse Core Ops, SparseCore 0:
  10.1 77.4 all-gather.2
  181.6 147.6 all-gather.4
where the time goes:
time: 601 us; the launch traced here: 599 us
  waiting for transfers between devices  421 us (70%)
  blocking collectives  59.8 us (10%)
  matrix products  32.3 us (5%)
  starting transfers between devices  27.6 us (5%)
  other arithmetic  27.2 us (5%)
  local copies, waits for them, and re-layouts  16.5 us (3%)
  between operations  14.6 us (2%)
    all_gather x1, waiting for transfers between devices, on_device(): lax.all_gather(out_grad, 'ctx', axis=0, tiled=True)  149 us
    all_to_all x1, waiting for transfers between devices, on_device(): lax.all_to_all(far_qgrad, 'ctx', split_axis=0, concat_axis=0, tiled=True)  148 us
    all_gather x1, waiting for transfers between devices, on_device(): lax.all_gather(queries, 'ctx', axis=0, tiled=True)  75.2 us
    all_gather x1, blocking collectives, on_device(): every_logsum = lax.all_gather(logsum, 'ctx', axis=0, tiled=True)  30.1 us
    all_gather x1, blocking collectives, on_device(): every_delta = lax.all_gather(deltas, 'ctx', axis=0, tiled=True)  29.7 us
    all_to_all x1, waiting for transfers between devices, on_device(): lax.all_to_all(far_output, 'ctx', split_axis=0, concat_axis=0, tiled=True)  28.2 us
    all_to_all x1, waiting for transfers between devices, on_device(): lax.all_to_all(far_total, 'ctx', split_axis=0, concat_axis=0, tiled=True)  12.5 us
  transfers between devices with their start and end apart: 6, of which 6 were waited for; matrix products, arithmetic and copies ran while one was open for 6% of the time, Pallas kernels for 0%

commit v1 on v0

v1 whole, which is shorter than its diff:
```python
import math

import jax
import jax.numpy as jnp
from jax import lax
from jax.experimental import pallas as pl
from jax.experimental.pallas import tpu as pltpu
from jax.sharding import PartitionSpec as P

N = 16
BLK = 128
DH = 128
HEADS = 4
ROWS = HEADS * 128
KEYS = 2 * BLK
SLOTS = 24
CB_DEV = 16
SCALE = 1.0 / math.sqrt(DH)
HIDDEN = -1e30
FLOOR = -1e25
WIDE = 2
FAR = 8
F32 = jnp.float32
BF16 = jnp.bfloat16
NT = (((1,), (1,)), ((), ()))
NN = (((1,), (0,)), ((), ()))


def dot(a, b, dims=NN):
    return lax.dot_general(a, b, dims, preferred_element_type=F32)


def wrap(x):
    return lax.rem(x + 2 * N, N)


def head(h):
    return slice(h * 128, (h + 1) * 128)


def pick_blocks(ids_ref, c, low):
    first = jnp.int32(CB_DEV)
    last = jnp.int32(-1)
    count = jnp.int32(0)
    for j in range(SLOTS):
        b = ids_ref[c, j] - low
        inside = (b >= 0) & (b < CB_DEV)
        first = jnp.where(inside, jnp.minimum(first, b), first)
        last = jnp.where(inside, jnp.maximum(last, b), last)
        count = count + jnp.where(inside, 1, 0)
    return jnp.minimum(first, CB_DEV - 1), jnp.maximum(last, 0), count


def ring_kernel(
    ids_ref, q_ref, k_ref, v_ref, ok_ref, ov_ref, g_ref,
    att_ref, qg_ref, okg_ref, ovg_ref, dks_ref, dvs_ref,
    q_all, g_all, nk, nv, lw, dp, ou, qu,
    own_lw, own_dp, own_ou, own_qu, own_st, own_del,
    st_out, st_in, del_out, del_in, lse_all, delta_all,
    ds_t, p_t, sb, rb, sf, rf,
    g_send, g_recv, c_send, c_recv, st_s, st_r, de_s, de_r, ls_s, ls_r, dl_s, dl_r,
):
    me = lax.axis_index("ctx")
    low = me * CB_DEV
    nbr = (wrap(me + 1), wrap(me - 1))

    barrier = pltpu.get_barrier_semaphore()

    def greet(p, _):
        pl.semaphore_signal(barrier, inc=1, device_id={"ctx": wrap(me + p)})
        return 0

    lax.fori_loop(1, N, greet, 0)
    for h in range(HEADS):
        q_all[me, head(h), :] = q_ref[:, head(h)]
        g_all[me, head(h), :] = g_ref[:, head(h)]
    pl.semaphore_wait(barrier, N - 1)

    def gather_copy(stream, D, t, half, c):
        buf = (q_all, g_all)[stream]
        part = buf.at[c, pl.ds(half * 256, 256)]
        return pltpu.make_async_remote_copy(
            src_ref=part, dst_ref=part,
            send_sem=g_send.at[stream, D, t - 1, half], recv_sem=g_recv.at[stream, D, t - 1, half],
            device_id={"ctx": nbr[D]},
        )

    def chunk_at(D, t):
        return wrap(me - t) if D == 0 else wrap(me + t)

    def gather_step(stream, t):
        for half in range(2):
            for D in range(2):
                steps = 8 if D == stream else 7
                if isinstance(t, int) and t > steps:
                    continue
                c = chunk_at(D, t)
                gather_copy(stream, D, t, half, c).wait_recv()
                if not isinstance(t, int) or t < steps:
                    gather_copy(stream, D, t + 1, half, c).start()

    def gather_first(stream):
        for half in range(2):
            for D in range(2):
                gather_copy(stream, D, 1, half, me).start()

    def gather_sent(stream, t):
        for half in range(2):
            for D in range(2):
                if isinstance(t, int) and t > (8 if D == stream else 7):
                    continue
                gather_copy(stream, D, t, half, me).wait_send()

    def to_candidate(src, dst, send, recv, c, slot):
        return pltpu.make_async_remote_copy(
            src_ref=src.at[c], dst_ref=dst.at[slot], send_sem=send.at[c], recv_sem=recv.at[slot],
            device_id={"ctx": c},
        )

    def to_holder(buf, send, recv, slot, p):
        return pltpu.make_async_remote_copy(
            src_ref=buf.at[slot], dst_ref=buf.at[slot], send_sem=send.at[p], recv_sem=recv.at[slot],
            device_id={"ctx": wrap(me + p)},
        )

    def each_peer(fn):
        def body(p, _):
            fn(p)
            return 0

        lax.fori_loop(1, N, body, 0)

    def scores(c):
        first, last, count = pick_blocks(ids_ref, c, low)
        nk[c, :BLK, :] = k_ref[first]
        nk[c, BLK:, :] = k_ref[last]
        nv[c, :BLK, :] = v_ref[first]
        nv[c, BLK:, :] = v_ref[last]
        bias0 = jnp.where(count >= 1, 0.0, HIDDEN).astype(F32)
        bias1 = jnp.where(count >= 2, 0.0, HIDDEN).astype(F32)
        keys = nk[c]
        vt = nv[c].T
        for h in range(HEADS):
            s = dot(keys, q_all[c, head(h), :], NT) * SCALE
            s0 = s[:BLK] + bias0
            s1 = s[BLK:] + bias1
            m = jnp.max(jnp.maximum(s0, s1), axis=0, keepdims=True)
            m = jnp.maximum(m, FLOOR)
            e = jnp.exp(jnp.concatenate([s0, s1], axis=0) - m)
            lw[c, :, head(h)] = e
            st_out[c, h : h + 1, :] = m
            st_out[c, HEADS + h : HEADS + h + 1, :] = jnp.sum(e, axis=0, keepdims=True)
            ou[c, :, head(h)] = dot(vt, e.astype(BF16))

    def send_scores(c):
        scores(c)
        to_candidate(st_out, st_in, st_s, st_r, c, me).start()

    def weights_grad(c):
        vals = nv[c]
        for h in range(HEADS):
            d = dot(vals, g_all[c, head(h), :], NT)
            dp[c, :, head(h)] = d
            e = lw[c, :, head(h)].astype(BF16).astype(F32)
            del_out[c, h : h + 1, :] = jnp.sum(e * d, axis=0, keepdims=True)

    def send_weights_grad(c):
        weights_grad(c)
        to_candidate(del_out, del_in, de_s, de_r, c, me).start()

    def grads(c):
        kt = nk[c].T
        f = jnp.exp(st_out[c, :HEADS, :] - lse_all[c, :HEADS, :])
        for h in range(HEADS):
            w = lw[c, :, head(h)] * f[h : h + 1, :]
            p_t[:, head(h)] = w.astype(BF16)
            ds = (w * (dp[c, :, head(h)] - delta_all[c, h : h + 1, :])).astype(BF16)
            ds_t[:, head(h)] = ds
            qu[c, :, head(h)] = dot(kt, ds)
        dks_ref[c] = dot(ds_t[...], q_all[c]) * SCALE
        dvs_ref[c] = dot(p_t[...], g_all[c])

    def own_scores():
        keys = ok_ref[...]
        vt = ov_ref[...].T
        seen = lax.broadcasted_iota(jnp.int32, (BLK, 128), 0) <= lax.broadcasted_iota(jnp.int32, (BLK, 128), 1)
        for h in range(HEADS):
            s = jnp.where(seen, dot(keys, q_all[me, head(h), :], NT) * SCALE, HIDDEN)
            m = jnp.max(s, axis=0, keepdims=True)
            e = jnp.exp(s - m)
            own_lw[:, head(h)] = e
            own_st[h : h + 1, :] = m
            own_st[HEADS + h : HEADS + h + 1, :] = jnp.sum(e, axis=0, keepdims=True)
            own_ou[:, head(h)] = dot(vt, e.astype(BF16))

    def own_weights_grad():
        vals = ov_ref[...]
        for h in range(HEADS):
            d = dot(vals, g_all[me, head(h), :], NT)
            own_dp[:, head(h)] = d
            e = own_lw[:, head(h)].astype(BF16).astype(F32)
            own_del[h : h + 1, :] = jnp.sum(e * d, axis=0, keepdims=True)

    def own_grads():
        kt = ok_ref[...].T
        f = jnp.exp(own_st[:HEADS, :] - lse_all[me, :HEADS, :])
        for h in range(HEADS):
            w = own_lw[:, head(h)] * f[h : h + 1, :]
            p_t[:BLK, head(h)] = w.astype(BF16)
            ds = (w * (own_dp[:, head(h)] - delta_all[me, h : h + 1, :])).astype(BF16)
            ds_t[:BLK, head(h)] = ds
            own_qu[:, head(h)] = dot(kt, ds)
        okg_ref[...] = (dot(ds_t[:BLK, :], q_all[me]) * SCALE).astype(BF16)
        ovg_ref[...] = dot(p_t[:BLK, :], g_all[me]).astype(BF16)

    def combine_logsum():
        st_in[me] = st_out[me]
        each_peer(lambda p: to_candidate(st_out, st_in, st_s, st_r, wrap(me + p), wrap(me + p)).wait_recv())
        maxima = st_in[:, :HEADS, :]
        totals = st_in[:, HEADS:, :]
        own_max = own_st[:HEADS, :]
        top = jnp.maximum(jnp.max(maxima, axis=0), own_max)
        total = own_st[HEADS:, :] * jnp.exp(own_max - top) + jnp.sum(totals * jnp.exp(maxima - top[None]), axis=0)
        lse_all[me, :HEADS, :] = top + jnp.log(total)
        each_peer(lambda p: to_holder(lse_all, ls_s, ls_r, me, p).start())

    def combine_deltas():
        del_in[me] = del_out[me]
        each_peer(lambda p: to_candidate(del_out, del_in, de_s, de_r, wrap(me + p), wrap(me + p)).wait_recv())
        logsum = lse_all[me, :HEADS, :]
        total = own_del[:HEADS, :] * jnp.exp(own_st[:HEADS, :] - logsum)
        total = total + jnp.sum(del_in[:, :HEADS, :] * jnp.exp(st_in[:, :HEADS, :] - logsum[None]), axis=0)
        delta_all[me, :HEADS, :] = total
        each_peer(lambda p: to_holder(delta_all, dl_s, dl_r, me, p).start())

    def buffers(chain, D, d):
        if isinstance(d, int) and d <= WIDE:
            return sf.at[chain, D, d - 1], rf.at[chain, D, d - 1]
        return sb.at[chain, D, d - 1 - WIDE], rb.at[chain, D, d - 1 - WIDE]

    def chain_copy(chain, D, d, half):
        src, dst = buffers(chain, D, d)
        rows = pl.ds(half * 64, 64)
        return pltpu.make_async_remote_copy(
            src_ref=src.at[rows], dst_ref=dst.at[rows],
            send_sem=c_send.at[chain, D, d - 1, half], recv_sem=c_recv.at[chain, D, d - 1, half],
            device_id={"ctx": nbr[D]},
        )

    def factor(c):
        return jnp.exp(st_out[c, :HEADS, :] - lse_all[c, :HEADS, :])

    def chain_step(chain, i):
        for half in range(2):
            rows = slice(half * 64, half * 64 + 64)
            for D in range(2):
                d = (8 if D == chain else 7) - i
                if isinstance(d, int) and d < 1:
                    continue
                c = wrap(me + d) if D == 0 else wrap(me - d)
                started = not isinstance(i, int) or i > 0
                if started:
                    chain_copy(chain, D, d + 1, half).wait_recv()
                    arrived = buffers(chain, D, d + 1)[1]
                out = buffers(chain, D, d)[0]
                f = factor(c) if chain == 0 else None
                for h in range(HEADS):
                    if chain == 0:
                        x = ou[c, rows, head(h)] * f[h : h + 1, :]
                    else:
                        x = qu[c, rows, head(h)]
                    if started:
                        x = x + arrived[rows, head(h)].astype(F32)
                    out[rows, head(h)] = x.astype(out.dtype)
                chain_copy(chain, D, d, half).start()

    def chain_sent(chain, i):
        for half in range(2):
            for D in range(2):
                d = (8 if D == chain else 7) - i
                if isinstance(d, int) and d < 1:
                    continue
                chain_copy(chain, D, d, half).wait_send()

    def chain_arrived(chain, D):
        for half in range(2):
            chain_copy(chain, D, 1, half).wait_recv()

    def chain_grads(i):
        for D in range(2):
            d = (8 if D == 1 else 7) - i
            if isinstance(d, int) and d < 1:
                continue
            grads(wrap(me + d) if D == 0 else wrap(me - d))

    def loop(lo, hi, fn):
        def body(t, _):
            fn(t)
            return 0

        lax.fori_loop(lo, hi, body, 0)

    gather_first(0)
    own_scores()
    scores(me)

    def query_step(t):
        gather_step(0, t)
        send_scores(chunk_at(0, t))
        send_scores(chunk_at(1, t))

    loop(1, 7, query_step)
    gather_step(0, 7)
    gather_first(1)
    send_scores(chunk_at(0, 7))
    send_scores(chunk_at(1, 7))
    gather_step(0, 8)
    send_scores(chunk_at(0, 8))

    def grad_step(t):
        gather_step(1, t)
        gather_sent(0, t)
        send_weights_grad(chunk_at(0, t))
        send_weights_grad(chunk_at(1, t))

    loop(1, 4, grad_step)
    combine_logsum()
    weights_grad(me)
    own_weights_grad()
    loop(4, 7, grad_step)
    gather_step(1, 7)
    each_peer(lambda p: to_holder(lse_all, ls_s, ls_r, wrap(me + p), p).wait_recv())
    chain_step(0, 0)
    gather_sent(0, 7)
    gather_sent(0, 8)
    send_weights_grad(chunk_at(0, 7))
    send_weights_grad(chunk_at(1, 7))
    gather_step(1, 8)
    send_weights_grad(chunk_at(1, 8))

    def output_step(i):
        chain_step(0, i)
        gather_sent(1, i)

    loop(1, 3, output_step)
    combine_deltas()
    loop(3, 5, output_step)
    each_peer(lambda p: to_candidate(st_out, st_in, st_s, st_r, wrap(me + p), me).wait_send())
    each_peer(lambda p: to_holder(lse_all, ls_s, ls_r, me, p).wait_send())
    chain_step(0, 5)
    for t in range(5, 9):
        gather_sent(1, t)
    each_peer(lambda p: to_holder(delta_all, dl_s, dl_r, wrap(me + p), p).wait_recv())
    chain_grads(0)
    chain_step(0, 6)
    chain_step(1, 0)
    chain_grads(1)
    chain_step(0, 7)

    def return_step(i):
        chain_step(1, i)
        chain_sent(0, i)
        chain_grads(i + 1)

    loop(1, 3, return_step)
    chain_arrived(0, 0)
    chain_arrived(0, 1)
    f_own = jnp.exp(own_st[:HEADS, :] - lse_all[me, :HEADS, :])
    f_me = factor(me)
    for h in range(HEADS):
        x = own_ou[:, head(h)] * f_own[h : h + 1, :] + ou[me, :, head(h)] * f_me[h : h + 1, :]
        x = x + rf[0, 0, 0, :, head(h)] + rf[0, 1, 0, :, head(h)]
        att_ref[:, head(h)] = x.T.astype(BF16)
    loop(3, 5, return_step)
    chain_step(1, 5)
    chain_grads(6)
    chain_sent(0, 0)
    for i in range(5, 8):
        chain_sent(0, i)
    chain_step(1, 6)
    chain_grads(7)
    chain_step(1, 7)
    grads(me)
    own_grads()
    each_peer(lambda p: to_candidate(del_out, del_in, de_s, de_r, wrap(me + p), me).wait_send())
    each_peer(lambda p: to_holder(delta_all, dl_s, dl_r, me, p).wait_send())
    for i in range(5):
        chain_sent(1, i)
    chain_arrived(1, 0)
    chain_arrived(1, 1)
    for h in range(HEADS):
        x = own_qu[:, head(h)] + qu[me, :, head(h)] + rf[1, 0, 0, :, head(h)] + rf[1, 1, 0, :, head(h)]
        qg_ref[:, head(h)] = (x * SCALE).T.astype(BF16)
    for i in range(5, 8):
        chain_sent(1, i)


def ring(ids, q, k, v, ok, ov, g):
    vm = pl.BlockSpec(memory_space=pltpu.VMEM)
    shape = jax.ShapeDtypeStruct
    V = pltpu.VMEM
    D = pltpu.SemaphoreType.DMA
    stats = V((N, 8, 128), F32)
    return pl.pallas_call(
        ring_kernel,
        in_specs=[pl.BlockSpec(memory_space=pltpu.SMEM)] + [vm] * 6,
        out_specs=[vm] * 6,
        out_shape=[
            shape((128, ROWS), BF16), shape((128, ROWS), BF16),
            shape((BLK, DH), BF16), shape((BLK, DH), BF16),
            shape((N, KEYS, DH), F32), shape((N, KEYS, DH), F32),
        ],
        scratch_shapes=[
            V((N, ROWS, DH), BF16), V((N, ROWS, DH), BF16),
            V((N, KEYS, DH), BF16), V((N, KEYS, DH), BF16),
            V((N, KEYS, ROWS), F32), V((N, KEYS, ROWS), F32),
            V((N, DH, ROWS), F32), V((N, DH, ROWS), F32),
            V((BLK, ROWS), F32), V((BLK, ROWS), F32), V((DH, ROWS), F32), V((DH, ROWS), F32),
            V((8, 128), F32), V((8, 128), F32),
            stats, stats, stats, stats, stats, stats,
            V((KEYS, ROWS), BF16), V((KEYS, ROWS), BF16),
            V((2, 2, FAR - WIDE, DH, ROWS), BF16), V((2, 2, FAR - WIDE, DH, ROWS), BF16),
            V((2, 2, WIDE, DH, ROWS), F32), V((2, 2, WIDE, DH, ROWS), F32),
            D((2, 2, 8, 2)), D((2, 2, 8, 2)), D((2, 2, 8, 2)), D((2, 2, 8, 2)),
            D((N,)), D((N,)), D((N,)), D((N,)), D((N,)), D((N,)), D((N,)), D((N,)),
        ],
        compiler_params=pltpu.CompilerParams(
            collective_id=0, has_side_effects=True, vmem_limit_bytes=60 * 1024 * 1024
        ),
        name="ring_attention",
    )(ids, q, k, v, ok, ov, g)


def sums_kernel(
    ids_ref, att_in, qg_in, okg_in, ovg_in, dks_ref, dvs_ref,
    att_ref, qg_ref, okg_ref, ovg_ref, dk_ref, dv_ref, dk, dv,
):
    low = lax.axis_index("ctx") * CB_DEV
    att_ref[...] = att_in[...]
    qg_ref[...] = qg_in[...]
    okg_ref[...] = okg_in[...]
    ovg_ref[...] = ovg_in[...]
    dk[...] = jnp.zeros_like(dk)
    dv[...] = jnp.zeros_like(dv)

    def add(c, _):
        first, last, count = pick_blocks(ids_ref, c, low)

        @pl.when(count >= 1)
        def _():
            dk[first] += dks_ref[c, :BLK, :]
            dv[first] += dvs_ref[c, :BLK, :]

        @pl.when(count >= 2)
        def _():
            dk[last] += dks_ref[c, BLK:, :]
            dv[last] += dvs_ref[c, BLK:, :]

        return 0

    lax.fori_loop(0, N, add, 0)
    dk_ref[...] = dk[...].astype(BF16)
    dv_ref[...] = dv[...].astype(BF16)


def sums(ids, *parts):
    vm = pl.BlockSpec(memory_space=pltpu.VMEM)
    shape = jax.ShapeDtypeStruct
    return pl.pallas_call(
        sums_kernel,
        in_specs=[pl.BlockSpec(memory_space=pltpu.SMEM)] + [vm] * 6,
        out_specs=[vm] * 6,
        out_shape=[
            shape((128, ROWS), BF16), shape((128, ROWS), BF16),
            shape((BLK, DH), BF16), shape((BLK, DH), BF16),
            shape((CB_DEV, BLK, DH), BF16), shape((CB_DEV, BLK, DH), BF16),
        ],
        scratch_shapes=[pltpu.VMEM((CB_DEV, BLK, DH), F32), pltpu.VMEM((CB_DEV, BLK, DH), F32)],
        compiler_params=pltpu.CompilerParams(vmem_limit_bytes=32 * 1024 * 1024),
        name="block_sums",
    )(ids, *parts)


def on_device(queries, context_keys, context_values, own_keys, own_values, out_grad, block_ids):
    k = context_keys.reshape(CB_DEV, BLK, DH)
    v = context_values.reshape(CB_DEV, BLK, DH)
    parts = ring(block_ids, queries, k, v, own_keys, own_values, out_grad)
    att, qg, okg, ovg, dk, dv = sums(block_ids, *parts)
    return att, qg, dk.reshape(CB_DEV * BLK, DH), dv.reshape(CB_DEV * BLK, DH), okg, ovg


def solution(mesh):
    rows = P(("dp", "ctx"), "head")
    return jax.shard_map(
        on_device,
        mesh=mesh,
        in_specs=(rows,) * 6 + (P("dp", None),),
        out_specs=(rows,) * 6,
        check_vma=False,
    )
```

time: 601 us -> 164 us (0.27)
  waiting for transfers between devices: 421 us -> 0 us
  Pallas kernels: 0 us -> 155 us
  blocking collectives: 59.8 us -> 0 us
  matrix products: 32.3 us -> 0 us
  starting transfers between devices: 27.6 us -> 0 us
  other arithmetic: 27.2 us -> 0 us
  between operations: 14.6 us -> 0.66 us
  local copies, waits for them, and re-layouts: 16.5 us -> 7.19 us
    all_gather x2 -> x0, waiting for transfers between devices: 224 us -> none  [the longest x1 149 us: on_device(): lax.all_gather(out_grad, 'ctx', axis=0, tiled=True)]
    all_to_all x4 -> x0, waiting for transfers between devices: 196 us -> none  [the longest x1 148 us: on_device(): lax.all_to_all(far_qgrad, 'ctx', split_axis=0, concat_axis=0, tiled=True)]
    pallas_call x0 -> x2, Pallas kernels: none -> 155 us  [the longest x1 151 us: ring(): pl.pallas_call(ring_kernel, in_specs=[pl.BlockSpec(memory_space=pltpu.SME...]
    all_gather x2 -> x0, blocking collectives: 59.8 us -> none  [the longest x1 30.1 us: on_device(): every_logsum = lax.all_gather(logsum, 'ctx', axis=0, tiled=True)]
    dot_general x12 -> x0, matrix products: 32.3 us -> none  [the longest x2 7.55 us: weighted_values(): jnp.einsum('bgrij,bjgd->bigrd', rounded, value_rows, preferred_element_ty...]
    all_to_all x4 -> x0, starting transfers between devices: 27.5 us -> none  [the longest x1 9.53 us: on_device(): lax.all_to_all(far_qgrad, 'ctx', split_axis=0, concat_axis=0, tiled=True)]
    reduce_sum x6 -> x0, other arithmetic: 11.7 us -> none  [the longest x2 5.98 us: partial_stats(): jnp.sum(jnp.where(visible, jnp.exp(scores - maxima[..., None]), 0.0), axi...]
    scatter-add x2 -> x0, other arithmetic: 9.33 us -> none  [block_sums(): return zero_sums.at[flat_index].add(jnp.where(flat_live, rows, 0.0))]
  transfers between devices with their start and end apart: 6 -> 0, of which waited for: 6 -> 0; matrix products, arithmetic and copies ran while one was open for 6% -> 0% of each run, Pallas kernels for 0% -> 0%
where the time goes in v1:
time: 164 us; the launch traced here: 163 us
  Pallas kernels  155 us (95%)
  local copies, waits for them, and re-layouts  7.19 us (4%)
    pallas_call x1, Pallas kernels, ring(): pl.pallas_call(ring_kernel, in_specs=[pl.BlockSpec(memory_space=pltpu.SME...  151 us
    unnamed x14, local copies, waits for them, and re-layouts  7.19 us
    pallas_call x1, Pallas kernels, sums(): pl.pallas_call(sums_kernel, in_specs=[pl.BlockSpec(memory_space=pltpu.SME...  4.04 us

profile of v1, /device:TPU:6, one launch (start us, length us, event | category | flops | bytes accessed | tf_op | source)
XLA Modules:
  0.0 163.1 jit_solution(17084483999040493427)
XLA Ops:
  0.6 151.2 %ring_attention.1 = (bf16[128,512]{1,0:T(8,128)(2,1)}, bf16[128,512]{1,0:T(8,128)(2,1)}, bf16[128,128]{1,0:T(8,128)(2,1)}, bf16[128,128]{1,0:T(8,128)(2,1)}, f32...) custom-call(s32[16,24]{1,0:T(8,128)} %ids_ref.3, bf16[128,512]{1,0:T(8,128)(2,1)} %q_ref.1, bf16[16,128,128]{2,1,0:T(8,128)(2,1)} %bitcast.4, ...), custom_call_target="tpu_custom_call" | custom-call | tf_op jit(solution)/shard_map/ring_attention/pallas_call | solution.py:404
  151.8 0.0 copy-start
  151.8 1.6 copy-done
  153.4 0.0 copy-start.1
  153.4 1.6 copy-done.1
  155.0 0.0 copy-start.2
  155.0 0.9 copy-done.2
  155.9 0.0 copy-start.3
  155.9 0.9 copy-done.3
  156.8 0.0 copy-start.4
  156.8 0.8 copy-done.4
  157.6 0.0 copy-start.5
  157.6 0.8 copy-done.5
  158.3 0.0 copy-start.6
  158.3 0.7 copy-done.6
  159.0 4.0 %block_sums.1 = (bf16[128,512]{1,0:T(8,128)(2,1)}, bf16[128,512]{1,0:T(8,128)(2,1)}, bf16[128,128]{1,0:T(8,128)(2,1)}, bf16[128,128]{1,0:T(8,128)(2,1)}, bf16[16...) custom-call(s32[16,24]{1,0:T(8,128)S(1)} %copy-done.6, bf16[128,512]{1,0:T(8,128)(2,1)S(1)} %copy-done.2, ...), custom_call_target="tpu_custom_call" | custom-call | tf_op jit(solution)/shard_map/block_sums/pallas_call | solution.py:469
Async XLA Ops:
  151.8 1.6 copy-start
  153.4 1.6 copy-start.1
  155.0 0.9 copy-start.2
  155.9 0.9 copy-start.3
  156.8 0.8 copy-start.4
  157.6 0.8 copy-start.5
  158.3 0.7 copy-start.6

commit v2 on v1

v2 whole, which is shorter than its diff:
```python
import math

import jax
import jax.numpy as jnp
from jax import lax
from jax.experimental import pallas as pl
from jax.experimental.pallas import tpu as pltpu
from jax.sharding import PartitionSpec as P

N = 16
BLK = 128
DH = 128
HEADS = 4
ROWS = HEADS * 128
KEYS = 2 * BLK
SLOTS = 24
CB_DEV = 16
EMPTY = 2 * N
SCALE = 1.0 / math.sqrt(DH)
HIDDEN = -1e30
FLOOR = -1e25
WIDE = 2
FAR = 8
F32 = jnp.float32
BF16 = jnp.bfloat16
NT = (((1,), (1,)), ((), ()))
NN = (((1,), (0,)), ((), ()))


def dot(a, b, dims=NN):
    return lax.dot_general(a, b, dims, preferred_element_type=F32)


def wrap(x):
    return lax.rem(x + 2 * N, N)


def head(h):
    return slice(h * 128, (h + 1) * 128)


def is_int(x):
    return isinstance(x, int)


def ring_kernel(
    ids_ref, q_ref, k_ref, v_ref, ok_ref, ov_ref, g_ref,
    att_ref, qg_ref, okg_ref, ovg_ref, dk_ref, dv_ref,
    q_all, g_all, nk, nv, lw, dp, ou, qu,
    own_lw, own_dp, own_ou, own_qu, own_st, own_del,
    st_out, st_in, del_out, del_in, lse_all, delta_all,
    ds_t, p_t, tr, dks, dvs, sel, sb, rb, sf, rf,
    g_send, g_recv, c_send, c_recv, st_s, st_r, de_s, de_r, ls_s, ls_r, dl_s, dl_r,
):
    me = lax.axis_index("ctx")
    low = me * CB_DEV
    nbr = (wrap(me + 1), wrap(me - 1))

    barrier = pltpu.get_barrier_semaphore()

    def loop(lo, hi, fn):
        def body(t, _):
            fn(t)
            return 0

        lax.fori_loop(lo, hi, body, 0)

    def each_peer(fn):
        loop(1, N, fn)

    each_peer(lambda p: pl.semaphore_signal(barrier, inc=1, device_id={"ctx": wrap(me + p)}))
    for h in range(HEADS):
        q_all[me, h] = q_ref[:, head(h)]
        g_all[me, h] = g_ref[:, head(h)]
    pl.semaphore_wait(barrier, N - 1)

    def gather_copy(stream, D, t, h, c):
        part = (q_all, g_all)[stream].at[c, h]
        return pltpu.make_async_remote_copy(
            src_ref=part, dst_ref=part,
            send_sem=g_send.at[stream, D, t - 1, h], recv_sem=g_recv.at[stream, D, t - 1, h],
            device_id={"ctx": nbr[D]},
        )

    def toward(D, d):
        return wrap(me + d) if D == 0 else wrap(me - d)

    def from_behind(D, t):
        return toward(1 - D, t)

    def gather_step(stream, t, work):
        for h in range(HEADS):
            for D in range(2):
                steps = 8 if D == stream else 7
                if is_int(t) and t > steps:
                    continue
                c = from_behind(D, t)
                gather_copy(stream, D, t, h, c).wait_recv()
                if not is_int(t) or t < steps:
                    gather_copy(stream, D, t + 1, h, c).start()
            work(h)

    def gather_first(stream):
        for h in range(HEADS):
            for D in range(2):
                gather_copy(stream, D, 1, h, me).start()

    def gather_sent(stream, t):
        for h in range(HEADS):
            for D in range(2):
                if is_int(t) and t > (8 if D == stream else 7):
                    continue
                gather_copy(stream, D, t, h, me).wait_send()

    def to_candidate(src, dst, send, recv, c, slot):
        return pltpu.make_async_remote_copy(
            src_ref=src.at[c], dst_ref=dst.at[slot], send_sem=send.at[c], recv_sem=recv.at[slot],
            device_id={"ctx": c},
        )

    def to_holder(buf, send, recv, slot, p):
        return pltpu.make_async_remote_copy(
            src_ref=buf.at[slot], dst_ref=buf.at[slot], send_sem=send.at[p], recv_sem=recv.at[slot],
            device_id={"ctx": wrap(me + p)},
        )

    def stage(c, D):
        first = jnp.int32(CB_DEV)
        last = jnp.int32(-1)
        count = jnp.int32(0)
        for j in range(SLOTS):
            b = ids_ref[c, j] - low
            inside = (b >= 0) & (b < CB_DEV)
            first = jnp.where(inside, jnp.minimum(first, b), first)
            last = jnp.where(inside, jnp.maximum(last, b), last)
            count = count + jnp.where(inside, 1, 0)
        sel[c, 0] = jnp.where(count >= 1, first, -1)
        sel[c, 1] = jnp.where(count >= 2, last, -1)
        first = jnp.minimum(first, CB_DEV - 1)
        last = jnp.maximum(last, 0)
        nk[c, :BLK, :] = k_ref[first]
        nk[c, BLK:, :] = k_ref[last]
        nv[c, :BLK, :] = v_ref[first]
        nv[c, BLK:, :] = v_ref[last]
        tr[D] = nv[c].T
        bias0 = jnp.where(count >= 1, 0.0, HIDDEN).astype(F32)
        bias1 = jnp.where(count >= 2, 0.0, HIDDEN).astype(F32)
        return bias0, bias1

    def scores(c, D, h, bias):
        s = dot(nk[c], q_all[c, h], NT) * SCALE
        s0 = s[:BLK] + bias[0]
        s1 = s[BLK:] + bias[1]
        m = jnp.max(jnp.maximum(s0, s1), axis=0, keepdims=True)
        m = jnp.maximum(m, FLOOR)
        e = jnp.exp(jnp.concatenate([s0, s1], axis=0) - m)
        lw[c, h] = e
        st_out[c, h : h + 1, :] = m
        st_out[c, HEADS + h : HEADS + h + 1, :] = jnp.sum(e, axis=0, keepdims=True)
        ou[c, h] = dot(tr[D], e.astype(BF16))

    def weights_grad(c, h):
        d = dot(nv[c], g_all[c, h], NT)
        dp[c, h] = d
        e = lw[c, h].astype(BF16).astype(F32)
        del_out[c, h : h + 1, :] = jnp.sum(e * d, axis=0, keepdims=True)

    def factor(c, h):
        return jnp.exp(st_out[c, h : h + 1, :] - lse_all[c, h : h + 1, :])

    def grads(c, D, h):
        if h == 0:
            tr[D] = nk[c].T
        w = lw[c, h] * factor(c, h)
        p_t[D, :, head(h)] = w.astype(BF16)
        ds = (w * (dp[c, h] - delta_all[c, h : h + 1, :])).astype(BF16)
        ds_t[D, :, head(h)] = ds
        qu[c, h] = dot(tr[D], ds)
        if h % 2 == 1:
            pair = slice((h - 1) * 128, (h + 1) * 128)
            a = dot(ds_t[D, :, pair], q_all[c, h - 1 : h + 1].reshape(256, DH))
            b = dot(p_t[D, :, pair], g_all[c, h - 1 : h + 1].reshape(256, DH))
            for slot in range(2):
                rows = slice(slot * BLK, (slot + 1) * BLK)
                if h == 1:
                    dks[2 * c + slot] = a[rows]
                    dvs[2 * c + slot] = b[rows]
                else:
                    dks[2 * c + slot] += a[rows]
                    dvs[2 * c + slot] += b[rows]

    def own_scores():
        keys = ok_ref[...]
        vt = ov_ref[...].T
        seen = lax.broadcasted_iota(jnp.int32, (BLK, 128), 0) <= lax.broadcasted_iota(jnp.int32, (BLK, 128), 1)
        for h in range(HEADS):
            s = jnp.where(seen, dot(keys, q_all[me, h], NT) * SCALE, HIDDEN)
            m = jnp.max(s, axis=0, keepdims=True)
            e = jnp.exp(s - m)
            own_lw[h] = e
            own_st[h : h + 1, :] = m
            own_st[HEADS + h : HEADS + h + 1, :] = jnp.sum(e, axis=0, keepdims=True)
            own_ou[h] = dot(vt, e.astype(BF16))

    def own_weights_grad(h):
        d = dot(ov_ref[...], g_all[me, h], NT)
        own_dp[h] = d
        e = own_lw[h].astype(BF16).astype(F32)
        own_del[h : h + 1, :] = jnp.sum(e * d, axis=0, keepdims=True)

    def own_factor(h):
        return jnp.exp(own_st[h : h + 1, :] - lse_all[me, h : h + 1, :])

    def own_grads(h):
        w = own_lw[h] * own_factor(h)
        p_t[2, :BLK, head(h)] = w.astype(BF16)
        ds = (w * (own_dp[h] - delta_all[me, h : h + 1, :])).astype(BF16)
        ds_t[2, :BLK, head(h)] = ds
        own_qu[h] = dot(ok_ref[...].T, ds)
        if h == HEADS - 1:
            okg_ref[...] = (dot(ds_t[2, :BLK, :], q_all[me].reshape(ROWS, DH)) * SCALE).astype(BF16)
            ovg_ref[...] = dot(p_t[2, :BLK, :], g_all[me].reshape(ROWS, DH)).astype(BF16)

    def combine_logsum():
        st_in[me] = st_out[me]
        each_peer(lambda p: to_candidate(st_out, st_in, st_s, st_r, wrap(me + p), wrap(me + p)).wait_recv())
        maxima = st_in[:, :HEADS, :]
        totals = st_in[:, HEADS:, :]
        own_max = own_st[:HEADS, :]
        top = jnp.maximum(jnp.max(maxima, axis=0), own_max)
        total = own_st[HEADS:, :] * jnp.exp(own_max - top) + jnp.sum(totals * jnp.exp(maxima - top[None]), axis=0)
        lse_all[me, :HEADS, :] = top + jnp.log(total)
        each_peer(lambda p: to_holder(lse_all, ls_s, ls_r, me, p).start())

    def combine_deltas():
        del_in[me] = del_out[me]
        each_peer(lambda p: to_candidate(del_out, del_in, de_s, de_r, wrap(me + p), wrap(me + p)).wait_recv())
        logsum = lse_all[me, :HEADS, :]
        total = own_del[:HEADS, :] * jnp.exp(own_st[:HEADS, :] - logsum)
        total = total + jnp.sum(del_in[:, :HEADS, :] * jnp.exp(st_in[:, :HEADS, :] - logsum[None]), axis=0)
        delta_all[me, :HEADS, :] = total
        each_peer(lambda p: to_holder(delta_all, dl_s, dl_r, me, p).start())

    def buffers(chain, D, d):
        if is_int(d) and d <= WIDE:
            return sf.at[chain, D, d - 1], rf.at[chain, D, d - 1]
        return sb.at[chain, D, d - 1 - WIDE], rb.at[chain, D, d - 1 - WIDE]

    def chain_copy(chain, D, d, h):
        src, dst = buffers(chain, D, d)
        return pltpu.make_async_remote_copy(
            src_ref=src.at[h], dst_ref=dst.at[h],
            send_sem=c_send.at[chain, D, d - 1, h], recv_sem=c_recv.at[chain, D, d - 1, h],
            device_id={"ctx": nbr[D]},
        )

    def dists(chain, i):
        for D in range(2):
            d = (8 if D == chain else 7) - i
            if not is_int(d) or d >= 1:
                yield D, d

    def chain_head(chain, i, h):
        for D, d in dists(chain, i):
            c = toward(D, d)
            x = ou[c, h] * factor(c, h) if chain == 0 else qu[c, h]
            if not is_int(i) or i > 0:
                chain_copy(chain, D, d + 1, h).wait_recv()
                x = x + buffers(chain, D, d + 1)[1][h].astype(F32)
            out = buffers(chain, D, d)[0]
            out[h] = x.astype(out.dtype)
            chain_copy(chain, D, d, h).start()

    def chain_step(chain, i, work=lambda h: None):
        for h in range(HEADS):
            chain_head(chain, i, h)
            work(h)

    def chain_sent(chain, i):
        for h in range(HEADS):
            for D, d in dists(chain, i):
                chain_copy(chain, D, d, h).wait_send()

    def chain_grads(i, h):
        for D, d in dists(1, i):
            grads(toward(D, d), D, h)

    def block_sum(b):
        a = jnp.zeros((BLK, DH), F32)
        g = jnp.zeros((BLK, DH), F32)
        for c in range(N):
            at = jnp.where(sel[c, 0] == b, 2 * c, jnp.where(sel[c, 1] == b, 2 * c + 1, EMPTY))
            a = a + dks[at]
            g = g + dvs[at]
        dk_ref[b] = (a * SCALE).astype(BF16)
        dv_ref[b] = g.astype(BF16)

    gather_first(0)
    own_scores()
    bias_me = stage(me, 0)
    for h in range(HEADS):
        scores(me, 0, h, bias_me)

    def query_step(t):
        bias = {}

        def work(h):
            for D in range(2):
                if is_int(t) and D == 1 and t > 7:
                    continue
                c = from_behind(D, t)
                if h == 0:
                    bias[D] = stage(c, D)
                scores(c, D, h, bias[D])
                if h == HEADS - 1:
                    to_candidate(st_out, st_in, st_s, st_r, c, me).start()

        gather_step(0, t, work)

    loop(1, 7, query_step)
    query_step(7)
    gather_first(1)
    query_step(8)

    def grad_step(t, then=lambda h: None):
        def work(h):
            for D in range(2):
                if is_int(t) and D == 0 and t > 7:
                    continue
                c = from_behind(D, t)
                weights_grad(c, h)
                if h == HEADS - 1:
                    to_candidate(del_out, del_in, de_s, de_r, c, me).start()
            then(h)

        gather_step(1, t, work)
        if not is_int(t):
            gather_sent(0, t)

    loop(1, 4, grad_step)
    combine_logsum()
    dks[EMPTY] = jnp.zeros((BLK, DH), F32)
    dvs[EMPTY] = jnp.zeros((BLK, DH), F32)

    def own_too(h):
        weights_grad(me, h)
        own_weights_grad(h)

    loop(4, 6, grad_step)
    grad_step(6, own_too)
    each_peer(lambda p: to_holder(lse_all, ls_s, ls_r, wrap(me + p), p).wait_recv())
    grad_step(7, lambda h: chain_head(0, 0, h))
    grad_step(8)

    def output_step(i):
        chain_step(0, i)
        gather_sent(1, i)

    loop(1, 3, output_step)
    combine_deltas()
    loop(3, 5, output_step)
    each_peer(lambda p: to_candidate(st_out, st_in, st_s, st_r, wrap(me + p), me).wait_send())
    each_peer(lambda p: to_holder(lse_all, ls_s, ls_r, me, p).wait_send())
    each_peer(lambda p: to_holder(delta_all, dl_s, dl_r, wrap(me + p), p).wait_recv())
    chain_step(0, 5, lambda h: chain_grads(0, h))

    def both(h):
        chain_head(1, 0, h)
        chain_grads(1, h)

    chain_step(0, 6, both)
    chain_step(0, 7, lambda h: chain_grads(2, h))

    def return_step(i):
        chain_step(1, i, lambda h: chain_grads(i + 2, h))

    loop(1, 5, return_step)

    def finish_output(h):
        x = own_ou[h] * own_factor(h) + ou[me, h] * factor(me, h)
        for D in range(2):
            chain_copy(0, D, 1, h).wait_recv()
            x = x + rf[0, D, 0, h]
        att_ref[:, head(h)] = x.T.astype(BF16)

    def step5(h):
        chain_grads(7, h)
        grads(me, 0, h)
        own_grads(h)
        finish_output(h)

    chain_step(1, 5, step5)

    def step6(h):
        block_sum(2 * h)
        block_sum(2 * h + 1)

    chain_step(1, 6, step6)

    def step7(h):
        block_sum(8 + 2 * h)
        block_sum(9 + 2 * h)

    chain_step(1, 7, step7)
    for t in range(6, 9):
        gather_sent(0, t)
    for t in range(5, 9):
        gather_sent(1, t)
    for i in range(8):
        chain_sent(0, i)
    each_peer(lambda p: to_candidate(del_out, del_in, de_s, de_r, wrap(me + p), me).wait_send())
    each_peer(lambda p: to_holder(delta_all, dl_s, dl_r, me, p).wait_send())
    for i in range(6):
        chain_sent(1, i)
    for h in range(HEADS):
        x = own_qu[h] + qu[me, h]
        for D in range(2):
            chain_copy(1, D, 1, h).wait_recv()
            x = x + rf[1, D, 0, h]
        qg_ref[:, head(h)] = (x * SCALE).T.astype(BF16)
    for i in range(6, 8):
        chain_sent(1, i)


def ring(ids, q, k, v, ok, ov, g):
    vm = pl.BlockSpec(memory_space=pltpu.VMEM)
    shape = jax.ShapeDtypeStruct
    V = pltpu.VMEM
    D = pltpu.SemaphoreType.DMA
    stats = V((N, 8, 128), F32)
    tile = (HEADS, 128, 128)
    return pl.pallas_call(
        ring_kernel,
        in_specs=[pl.BlockSpec(memory_space=pltpu.SMEM)] + [vm] * 6,
        out_specs=[vm] * 6,
        out_shape=[
            shape((128, ROWS), BF16), shape((128, ROWS), BF16),
            shape((BLK, DH), BF16), shape((BLK, DH), BF16),
            shape((CB_DEV, BLK, DH), BF16), shape((CB_DEV, BLK, DH), BF16),
        ],
        scratch_shapes=[
            V((N,) + tile, BF16), V((N,) + tile, BF16),
            V((N, KEYS, DH), BF16), V((N, KEYS, DH), BF16),
            V((N, HEADS, KEYS, 128), F32), V((N, HEADS, KEYS, 128), F32),
            V((N,) + tile, F32), V((N,) + tile, F32),
            V(tile, F32), V(tile, F32), V(tile, F32), V(tile, F32),
            V((8, 128), F32), V((8, 128), F32),
            stats, stats, stats, stats, stats, stats,
            V((3, KEYS, ROWS), BF16), V((3, KEYS, ROWS), BF16), V((2, DH, KEYS), BF16),
            V((2 * N + 1, BLK, DH), F32), V((2 * N + 1, BLK, DH), F32),
            pltpu.SMEM((N, 2), jnp.int32),
            V((2, 2, FAR - WIDE) + tile, BF16), V((2, 2, FAR - WIDE) + tile, BF16),
            V((2, 2, WIDE) + tile, F32), V((2, 2, WIDE) + tile, F32),
            D((2, 2, 8, HEADS)), D((2, 2, 8, HEADS)), D((2, 2, 8, HEADS)), D((2, 2, 8, HEADS)),
            D((N,)), D((N,)), D((N,)), D((N,)), D((N,)), D((N,)), D((N,)), D((N,)),
        ],
        compiler_params=pltpu.CompilerParams(
            collective_id=0, has_side_effects=True, vmem_limit_bytes=60 * 1024 * 1024
        ),
        name="ring_attention",
    )(ids, q, k, v, ok, ov, g)


def hand_on_kernel(*refs):
    n = len(refs) // 2
    copies = [pltpu.make_async_copy(refs[j], refs[n + j], refs[2 * n].at[j]) for j in range(n)]
    for copy in copies:
        copy.start()
    for copy in copies:
        copy.wait()


def hand_on(parts):
    hbm = pl.BlockSpec(memory_space=pl.ANY)
    return pl.pallas_call(
        hand_on_kernel,
        in_specs=[hbm] * len(parts),
        out_specs=[hbm] * len(parts),
        out_shape=[jax.ShapeDtypeStruct(x.shape, x.dtype) for x in parts],
        scratch_shapes=[pltpu.SemaphoreType.DMA((len(parts),))],
        compiler_params=pltpu.CompilerParams(vmem_limit_bytes=60 * 1024 * 1024),
        name="hand_on",
    )(*parts)


def on_device(queries, context_keys, context_values, own_keys, own_values, out_grad, block_ids):
    k = context_keys.reshape(CB_DEV, BLK, DH)
    v = context_values.reshape(CB_DEV, BLK, DH)
    parts = ring(block_ids, queries, k, v, own_keys, own_values, out_grad)
    att, qg, okg, ovg, dk, dv = hand_on(parts)
    return att, qg, dk.reshape(CB_DEV * BLK, DH), dv.reshape(CB_DEV * BLK, DH), okg, ovg


def solution(mesh):
    rows = P(("dp", "ctx"), "head")
    return jax.shard_map(
        on_device,
        mesh=mesh,
        in_specs=(rows,) * 6 + (P("dp", None),),
        out_specs=(rows,) * 6,
        check_vma=False,
    )
```

time: 164 us -> 189 us (1.15)
  Pallas kernels: 155 us -> 188 us
  local copies, waits for them, and re-layouts: 7.19 us -> 0 us
    pallas_call x1, Pallas kernels: 4.04 us -> 42.8 us  [hand_on(): pl.pallas_call(hand_on_kernel, in_specs=[hbm] * len(parts), out_specs=[hb...]
    unnamed x14 -> x0, local copies, waits for them, and re-layouts: 7.19 us -> none
    pallas_call x1, Pallas kernels: 151 us -> 145 us  [ring(): pl.pallas_call(ring_kernel, in_specs=[pl.BlockSpec(memory_space=pltpu.SME...]
where the time goes in v2:
time: 189 us
  Pallas kernels  188 us (99%)
    pallas_call x1, Pallas kernels, ring(): pl.pallas_call(ring_kernel, in_specs=[pl.BlockSpec(memory_space=pltpu.SME...  145 us
    pallas_call x1, Pallas kernels, hand_on(): pl.pallas_call(hand_on_kernel, in_specs=[hbm] * len(parts), out_specs=[hb...  42.8 us

profile of v2, /device:TPU:6, one launch (start us, length us, event | category | flops | bytes accessed | tf_op | source)
XLA Modules:
  0.0 188.9 jit_solution(488320307831936280)
XLA Ops:
  0.6 145.3 %ring_attention.1 = (bf16[128,512]{1,0:T(8,128)(2,1)}, bf16[128,512]{1,0:T(8,128)(2,1)}, bf16[128,128]{1,0:T(8,128)(2,1)}, bf16[128,128]{1,0:T(8,128)(2,1)}, bf1...) custom-call(s32[16,24]{1,0:T(8,128)} %ids_ref.1, bf16[128,512]{1,0:T(8,128)(2,1)} %q_ref.1, ...), custom_call_target="tpu_custom_call" | custom-call | tf_op jit(solution)/shard_map/ring_attention/pallas_call | solution.py:432
  145.9 42.8 %hand_on.1 = (bf16[128,512]{1,0:T(8,128)(2,1)}, bf16[128,512]{1,0:T(8,128)(2,1)}, bf16[128,128]{1,0:T(8,128)(2,1)}, bf16[128,128]{1,0:T(8,128)(2,1)}, bf16[16,12...) custom-call(bf16[128,512]{1,0:T(8,128)(2,1)} %get-tuple-element.18.refs_0_, ...), custom_call_target="tpu_custom_call" | custom-call | tf_op jit(solution)/shard_map/hand_on/pallas_call | solution.py:475

commit v3 on v2

--- a/solution.py
+++ b/solution.py
@@ -21,6 +21,7 @@
 FLOOR = -1e25
 WIDE = 2
 FAR = 8
+LAG = 2
 F32 = jnp.float32
 BF16 = jnp.bfloat16
 NT = (((1,), (1,)), ((), ()))
@@ -88,22 +89,19 @@
     def from_behind(D, t):
         return toward(1 - D, t)
 
-    def gather_step(stream, t, work):
-        for h in range(HEADS):
-            for D in range(2):
-                steps = 8 if D == stream else 7
-                if is_int(t) and t > steps:
-                    continue
-                c = from_behind(D, t)
-                gather_copy(stream, D, t, h, c).wait_recv()
-                if not is_int(t) or t < steps:
-                    gather_copy(stream, D, t + 1, h, c).start()
-            work(h)
-
-    def gather_first(stream):
-        for h in range(HEADS):
-            for D in range(2):
-                gather_copy(stream, D, 1, h, me).start()
+    def gather_head(stream, t, h):
+        for D in range(2):
+            steps = 8 if D == stream else 7
+            if is_int(t) and t > steps:
+                continue
+            c = from_behind(D, t)
+            gather_copy(stream, D, t, h, c).wait_recv()
+            if not is_int(t) or t < steps:
+                gather_copy(stream, D, t + 1, h, c).start()
+
+    def gather_first(stream, h):
+        for D in range(2):
+            gather_copy(stream, D, 1, h, me).start()
 
     def gather_sent(stream, t):
         for h in range(HEADS):
@@ -271,11 +269,6 @@
             out[h] = x.astype(out.dtype)
             chain_copy(chain, D, d, h).start()
 
-    def chain_step(chain, i, work=lambda h: None):
-        for h in range(HEADS):
-            chain_head(chain, i, h)
-            work(h)
-
     def chain_sent(chain, i):
         for h in range(HEADS):
             for D, d in dists(chain, i):
@@ -295,121 +288,115 @@
         dk_ref[b] = (a * SCALE).astype(BF16)
         dv_ref[b] = g.astype(BF16)
 
-    gather_first(0)
+    def query_work(t, bias, h):
+        for D in range(2):
+            if is_int(t) and D == 1 and t > 7:
+                continue
+            c = from_behind(D, t)
+            if h == 0:
+                bias[D] = stage(c, D)
+            scores(c, D, h, bias[D])
+            if h == HEADS - 1:
+                to_candidate(st_out, st_in, st_s, st_r, c, me).start()
+
+    def grad_work(t, h):
+        for D in range(2):
+            if is_int(t) and D == 0 and t > 7:
+                continue
+            c = from_behind(D, t)
+            weights_grad(c, h)
+            if h == HEADS - 1:
+                to_candidate(del_out, del_in, de_s, de_r, c, me).start()
+
+    def gather_slot(s, extra=lambda h: None):
+        bias = {}
+        for h in range(HEADS):
+            if not is_int(s) or s <= 8:
+                gather_head(0, s, h)
+            if not is_int(s) or s > LAG:
+                gather_head(1, s - LAG, h)
+            elif s == LAG:
+                gather_first(1, h)
+            if not is_int(s) or s <= 8:
+                query_work(s, bias, h)
+            if not is_int(s) or s > LAG:
+                grad_work(s - LAG, h)
+            extra(h)
+
+    for h in range(HEADS):
+        gather_first(0, h)
     own_scores()
     bias_me = stage(me, 0)
     for h in range(HEADS):
         scores(me, 0, h, bias_me)
-
-    def query_step(t):
-        bias = {}
-
-        def work(h):
-            for D in range(2):
-                if is_int(t) and D == 1 and t > 7:
-                    continue
-                c = from_behind(D, t)
-                if h == 0:
-                    bias[D] = stage(c, D)
-                scores(c, D, h, bias[D])
-                if h == HEADS - 1:
-                    to_candidate(st_out, st_in, st_s, st_r, c, me).start()
-
-        gather_step(0, t, work)
-
-    loop(1, 7, query_step)
-    query_step(7)
-    gather_first(1)
-    query_step(8)
-
-    def grad_step(t, then=lambda h: None):
-        def work(h):
-            for D in range(2):
-                if is_int(t) and D == 0 and t > 7:
-                    continue
-                c = from_behind(D, t)
-                weights_grad(c, h)
-                if h == HEADS - 1:
-                    to_candidate(del_out, del_in, de_s, de_r, c, me).start()
-            then(h)
-
-        gather_step(1, t, work)
-        if not is_int(t):
-            gather_sent(0, t)
-
-    loop(1, 4, grad_step)
-    combine_logsum()
-    dks[EMPTY] = jnp.zeros((BLK, DH), F32)
-    dvs[EMPTY] = jnp.zeros((BLK, DH), F32)
+    for s in range(1, LAG + 1):
+        gather_slot(s)
+    loop(LAG + 1, 7, gather_slot)
 
     def own_too(h):
         weights_grad(me, h)
         own_weights_grad(h)
 
-    loop(4, 6, grad_step)
-    grad_step(6, own_too)
+    dks[EMPTY] = jnp.zeros((BLK, DH), F32)
+    dvs[EMPTY] = jnp.zeros((BLK, DH), F32)
+    gather_slot(7)
+    gather_slot(8)
+    for s in range(9, 8 + LAG):
+        gather_slot(s, own_too if s == 9 else lambda h: None)
+    combine_logsum()
+    gather_slot(8 + LAG)
     each_peer(lambda p: to_holder(lse_all, ls_s, ls_r, wrap(me + p), p).wait_recv())
-    grad_step(7, lambda h: chain_head(0, 0, h))
-    grad_step(8)
-
-    def output_step(i):
-        chain_step(0, i)
-        gather_sent(1, i)
-
-    loop(1, 3, output_step)
+
+    for h in range(HEADS):
+        chain_head(0, 0, h)
+    for t in range(1, 5):
+        gather_sent(0, t)
+    for h in range(HEADS):
+        chain_head(0, 1, h)
+    for t in range(5, 9):
+        gather_sent(0, t)
     combine_deltas()
-    loop(3, 5, output_step)
+    for h in range(HEADS):
+        chain_head(0, 2, h)
+    each_peer(lambda p: to_holder(delta_all, dl_s, dl_r, wrap(me + p), p).wait_recv())
+    for h in range(HEADS):
+        chain_grads(0, h)
+        chain_head(1, 0, h)
+    for h in range(HEADS):
+        chain_grads(1, h)
+
+    def chain_slot(u):
+        for h in range(HEADS):
+            if not is_int(u) or u < 8:
+                chain_head(0, u, h)
+            chain_head(1, u - 2, h)
+            chain_grads(u - 1, h)
+
+    loop(3, 5, chain_slot)
+    chain_slot(5)
+    for t in range(1, 9):
+        gather_sent(1, t)
+    chain_slot(6)
     each_peer(lambda p: to_candidate(st_out, st_in, st_s, st_r, wrap(me + p), me).wait_send())
     each_peer(lambda p: to_holder(lse_all, ls_s, ls_r, me, p).wait_send())
-    each_peer(lambda p: to_holder(delta_all, dl_s, dl_r, wrap(me + p), p).wait_recv())
-    chain_step(0, 5, lambda h: chain_grads(0, h))
-
-    def both(h):
-        chain_head(1, 0, h)
-        chain_grads(1, h)
-
-    chain_step(0, 6, both)
-    chain_step(0, 7, lambda h: chain_grads(2, h))
-
-    def return_step(i):
-        chain_step(1, i, lambda h: chain_grads(i + 2, h))
-
-    loop(1, 5, return_step)
-
-    def finish_output(h):
+    chain_slot(7)
+    each_peer(lambda p: to_candidate(del_out, del_in, de_s, de_r, wrap(me + p), me).wait_send())
+    each_peer(lambda p: to_holder(delta_all, dl_s, dl_r, me, p).wait_send())
+    for h in range(HEADS):
+        chain_head(1, 6, h)
+        chain_grads(7, h)
+        grads(me, 0, h)
+        own_grads(h)
+    for h in range(HEADS):
         x = own_ou[h] * own_factor(h) + ou[me, h] * factor(me, h)
         for D in range(2):
             chain_copy(0, D, 1, h).wait_recv()
             x = x + rf[0, D, 0, h]
         att_ref[:, head(h)] = x.T.astype(BF16)
-
-    def step5(h):
-        chain_grads(7, h)
-        grads(me, 0, h)
-        own_grads(h)
-        finish_output(h)
-
-    chain_step(1, 5, step5)
-
-    def step6(h):
-        block_sum(2 * h)
-        block_sum(2 * h + 1)
-
-    chain_step(1, 6, step6)
-
-    def step7(h):
-        block_sum(8 + 2 * h)
-        block_sum(9 + 2 * h)
-
-    chain_step(1, 7, step7)
-    for t in range(6, 9):
-        gather_sent(0, t)
-    for t in range(5, 9):
-        gather_sent(1, t)
+        chain_head(1, 7, h)
+    loop(0, CB_DEV, block_sum)
     for i in range(8):
         chain_sent(0, i)
-    each_peer(lambda p: to_candidate(del_out, del_in, de_s, de_r, wrap(me + p), me).wait_send())
-    each_peer(lambda p: to_holder(delta_all, dl_s, dl_r, me, p).wait_send())
     for i in range(6):
         chain_sent(1, i)
     for h in range(HEADS):
@@ -463,21 +450,17 @@
 
 def hand_on_kernel(*refs):
     n = len(refs) // 2
-    copies = [pltpu.make_async_copy(refs[j], refs[n + j], refs[2 * n].at[j]) for j in range(n)]
-    for copy in copies:
-        copy.start()
-    for copy in copies:
-        copy.wait()
+    for j in range(n):
+        refs[n + j][...] = refs[j][...]
 
 
 def hand_on(parts):
-    hbm = pl.BlockSpec(memory_space=pl.ANY)
+    vm = pl.BlockSpec(memory_space=pltpu.VMEM)
     return pl.pallas_call(
         hand_on_kernel,
-        in_specs=[hbm] * len(parts),
-        out_specs=[hbm] * len(parts),
+        in_specs=[vm] * len(parts),
+        out_specs=[vm] * len(parts),
         out_shape=[jax.ShapeDtypeStruct(x.shape, x.dtype) for x in parts],
-        scratch_shapes=[pltpu.SemaphoreType.DMA((len(parts),))],
         compiler_params=pltpu.CompilerParams(vmem_limit_bytes=60 * 1024 * 1024),
         name="hand_on",
     )(*parts)

time: 189 us -> 148 us (0.78)
  Pallas kernels: 188 us -> 147 us
    pallas_call x1, Pallas kernels: 42.8 us -> 2.46 us  [hand_on(): pl.pallas_call(hand_on_kernel, in_specs=[vm] * len(parts), out_specs=[vm]...]
where the time goes in v3:
time: 148 us; the launch traced here: 147 us
  Pallas kernels  147 us (99%)
    pallas_call x1, Pallas kernels, ring(): pl.pallas_call(ring_kernel, in_specs=[pl.BlockSpec(memory_space=pltpu.SME...  144 us

profile of v3, /device:TPU:6, one launch (start us, length us, event | category | flops | bytes accessed | tf_op | source)
XLA Modules:
  0.0 147.5 jit_solution(5194479007027506035)
XLA Ops:
  0.6 144.4 %ring_attention.1 = (bf16[128,512]{1,0:T(8,128)(2,1)}, bf16[128,512]{1,0:T(8,128)(2,1)}, bf16[128,128]{1,0:T(8,128)(2,1)}, bf16[128,128]{1,0:T(8,128)(2,1)}, bf1...) custom-call(s32[16,24]{1,0:T(8,128)} %ids_ref.1, bf16[128,512]{1,0:T(8,128)(2,1)} %q_ref.1, ...), custom_call_target="tpu_custom_call" | custom-call | tf_op jit(solution)/shard_map/ring_attention/pallas_call | solution.py:419
  145.0 2.5 %hand_on.1 = (bf16[128,512]{1,0:T(8,128)(2,1)}, bf16[128,512]{1,0:T(8,128)(2,1)}, bf16[128,128]{1,0:T(8,128)(2,1)}, bf16[128,128]{1,0:T(8,128)(2,1)}, bf16[16,12...) custom-call(bf16[128,512]{1,0:T(8,128)(2,1)} %get-tuple-element.18.refs_0_, ...), custom_call_target="tpu_custom_call" | custom-call | tf_op jit(solution)/shard_map/hand_on/pallas_call | solution.py:459

commit v4 on v3

--- a/solution.py
+++ b/solution.py
@@ -49,7 +49,7 @@
     att_ref, qg_ref, okg_ref, ovg_ref, dk_ref, dv_ref,
     q_all, g_all, nk, nv, lw, dp, ou, qu,
     own_lw, own_dp, own_ou, own_qu, own_st, own_del,
-    st_out, st_in, del_out, del_in, lse_all, delta_all,
+    st_out, st_in, del_out, del_in, lse_all, delta_all, fac,
     ds_t, p_t, tr, dks, dvs, sel, sb, rb, sf, rf,
     g_send, g_recv, c_send, c_recv, st_s, st_r, de_s, de_r, ls_s, ls_r, dl_s, dl_r,
 ):
@@ -75,11 +75,11 @@
         g_all[me, h] = g_ref[:, head(h)]
     pl.semaphore_wait(barrier, N - 1)
 
-    def gather_copy(stream, D, t, h, c):
-        part = (q_all, g_all)[stream].at[c, h]
+    def gather_copy(stream, D, t, b, c):
+        part = (q_all, g_all)[stream].at[c, pl.ds(2 * b, 2)]
         return pltpu.make_async_remote_copy(
             src_ref=part, dst_ref=part,
-            send_sem=g_send.at[stream, D, t - 1, h], recv_sem=g_recv.at[stream, D, t - 1, h],
+            send_sem=g_send.at[stream, D, t - 1, b], recv_sem=g_recv.at[stream, D, t - 1, b],
             device_id={"ctx": nbr[D]},
         )
 
@@ -89,26 +89,30 @@
     def from_behind(D, t):
         return toward(1 - D, t)
 
-    def gather_head(stream, t, h):
-        for D in range(2):
-            steps = 8 if D == stream else 7
-            if is_int(t) and t > steps:
-                continue
-            c = from_behind(D, t)
-            gather_copy(stream, D, t, h, c).wait_recv()
-            if not is_int(t) or t < steps:
-                gather_copy(stream, D, t + 1, h, c).start()
-
-    def gather_first(stream, h):
-        for D in range(2):
-            gather_copy(stream, D, 1, h, me).start()
+    def ways(d, b):
+        return (b,) if is_int(d) and d == FAR else () if is_int(d) and d > FAR else (0, 1)
+
+    def behind(t):
+        if is_int(t) and t == FAR:
+            return ((wrap(me + FAR), 0),)
+        return ((from_behind(0, t), 0), (from_behind(1, t), 1))
+
+    def gather_step(stream, t):
+        for b in range(2):
+            for D in ways(t, b):
+                gather_copy(stream, D, t, b, from_behind(D, t)).wait_recv()
+            for D in ways(t + 1, b):
+                gather_copy(stream, D, t + 1, b, from_behind(D, t)).start()
+
+    def gather_first(stream):
+        for b in range(2):
+            for D in range(2):
+                gather_copy(stream, D, 1, b, me).start()
 
     def gather_sent(stream, t):
-        for h in range(HEADS):
-            for D in range(2):
-                if is_int(t) and t > (8 if D == stream else 7):
-                    continue
-                gather_copy(stream, D, t, h, me).wait_send()
+        for b in range(2):
+            for D in ways(t, b):
+                gather_copy(stream, D, t, b, me).wait_send()
 
     def to_candidate(src, dst, send, recv, c, slot):
         return pltpu.make_async_remote_copy(
@@ -163,29 +167,20 @@
         e = lw[c, h].astype(BF16).astype(F32)
         del_out[c, h : h + 1, :] = jnp.sum(e * d, axis=0, keepdims=True)
 
-    def factor(c, h):
-        return jnp.exp(st_out[c, h : h + 1, :] - lse_all[c, h : h + 1, :])
-
-    def grads(c, D, h):
-        if h == 0:
-            tr[D] = nk[c].T
-        w = lw[c, h] * factor(c, h)
-        p_t[D, :, head(h)] = w.astype(BF16)
-        ds = (w * (dp[c, h] - delta_all[c, h : h + 1, :])).astype(BF16)
-        ds_t[D, :, head(h)] = ds
-        qu[c, h] = dot(tr[D], ds)
-        if h % 2 == 1:
-            pair = slice((h - 1) * 128, (h + 1) * 128)
-            a = dot(ds_t[D, :, pair], q_all[c, h - 1 : h + 1].reshape(256, DH))
-            b = dot(p_t[D, :, pair], g_all[c, h - 1 : h + 1].reshape(256, DH))
-            for slot in range(2):
-                rows = slice(slot * BLK, (slot + 1) * BLK)
-                if h == 1:
-                    dks[2 * c + slot] = a[rows]
-                    dvs[2 * c + slot] = b[rows]
-                else:
-                    dks[2 * c + slot] += a[rows]
-                    dvs[2 * c + slot] += b[rows]
+    def grads(c, D):
+        tr[D] = nk[c].T
+        for h in range(HEADS):
+            w = lw[c, h] * fac[c, h : h + 1, :]
+            p_t[D, :, head(h)] = w.astype(BF16)
+            ds = (w * (dp[c, h] - delta_all[c, h : h + 1, :])).astype(BF16)
+            ds_t[D, :, head(h)] = ds
+            qu[c, h] = dot(tr[D], ds)
+        a = dot(ds_t[D], q_all[c].reshape(ROWS, DH))
+        b = dot(p_t[D], g_all[c].reshape(ROWS, DH))
+        for slot in range(2):
+            rows = slice(slot * BLK, (slot + 1) * BLK)
+            dks[2 * c + slot] = a[rows]
+            dvs[2 * c + slot] = b[rows]
 
     def own_scores():
         keys = ok_ref[...]
@@ -209,15 +204,16 @@
     def own_factor(h):
         return jnp.exp(own_st[h : h + 1, :] - lse_all[me, h : h + 1, :])
 
-    def own_grads(h):
-        w = own_lw[h] * own_factor(h)
-        p_t[2, :BLK, head(h)] = w.astype(BF16)
-        ds = (w * (own_dp[h] - delta_all[me, h : h + 1, :])).astype(BF16)
-        ds_t[2, :BLK, head(h)] = ds
-        own_qu[h] = dot(ok_ref[...].T, ds)
-        if h == HEADS - 1:
-            okg_ref[...] = (dot(ds_t[2, :BLK, :], q_all[me].reshape(ROWS, DH)) * SCALE).astype(BF16)
-            ovg_ref[...] = dot(p_t[2, :BLK, :], g_all[me].reshape(ROWS, DH)).astype(BF16)
+    def own_grads():
+        kt = ok_ref[...].T
+        for h in range(HEADS):
+            w = own_lw[h] * own_factor(h)
+            p_t[2, :BLK, head(h)] = w.astype(BF16)
+            ds = (w * (own_dp[h] - delta_all[me, h : h + 1, :])).astype(BF16)
+            ds_t[2, :BLK, head(h)] = ds
+            own_qu[h] = dot(kt, ds)
+        okg_ref[...] = (dot(ds_t[2, :BLK, :], q_all[me].reshape(ROWS, DH)) * SCALE).astype(BF16)
+        ovg_ref[...] = dot(p_t[2, :BLK, :], g_all[me].reshape(ROWS, DH)).astype(BF16)
 
     def combine_logsum():
         st_in[me] = st_out[me]
@@ -244,39 +240,41 @@
             return sf.at[chain, D, d - 1], rf.at[chain, D, d - 1]
         return sb.at[chain, D, d - 1 - WIDE], rb.at[chain, D, d - 1 - WIDE]
 
-    def chain_copy(chain, D, d, h):
+    def chain_copy(chain, D, d, b):
         src, dst = buffers(chain, D, d)
         return pltpu.make_async_remote_copy(
-            src_ref=src.at[h], dst_ref=dst.at[h],
-            send_sem=c_send.at[chain, D, d - 1, h], recv_sem=c_recv.at[chain, D, d - 1, h],
+            src_ref=src.at[pl.ds(2 * b, 2)], dst_ref=dst.at[pl.ds(2 * b, 2)],
+            send_sem=c_send.at[chain, D, d - 1, b], recv_sem=c_recv.at[chain, D, d - 1, b],
             device_id={"ctx": nbr[D]},
         )
 
-    def dists(chain, i):
-        for D in range(2):
-            d = (8 if D == chain else 7) - i
-            if not is_int(d) or d >= 1:
-                yield D, d
-
-    def chain_head(chain, i, h):
-        for D, d in dists(chain, i):
-            c = toward(D, d)
-            x = ou[c, h] * factor(c, h) if chain == 0 else qu[c, h]
-            if not is_int(i) or i > 0:
-                chain_copy(chain, D, d + 1, h).wait_recv()
-                x = x + buffers(chain, D, d + 1)[1][h].astype(F32)
-            out = buffers(chain, D, d)[0]
-            out[h] = x.astype(out.dtype)
-            chain_copy(chain, D, d, h).start()
+    def chain_step(chain, i):
+        d = FAR - i
+        for b in range(2):
+            for D in ways(d + 1, b):
+                chain_copy(chain, D, d + 1, b).wait_recv()
+            for D in ways(d, b):
+                c = toward(D, d)
+                out = buffers(chain, D, d)[0]
+                for h in (2 * b, 2 * b + 1):
+                    x = ou[c, h] * fac[c, h : h + 1, :] if chain == 0 else qu[c, h]
+                    if D in ways(d + 1, b):
+                        x = x + buffers(chain, D, d + 1)[1][h].astype(F32)
+                    out[h] = x.astype(out.dtype)
+            for D in ways(d, b):
+                chain_copy(chain, D, d, b).start()
 
     def chain_sent(chain, i):
-        for h in range(HEADS):
-            for D, d in dists(chain, i):
-                chain_copy(chain, D, d, h).wait_send()
-
-    def chain_grads(i, h):
-        for D, d in dists(1, i):
-            grads(toward(D, d), D, h)
+        for b in range(2):
+            for D in ways(FAR - i, b):
+                chain_copy(chain, D, FAR - i, b).wait_send()
+
+    def chain_grads(i):
+        if is_int(i) and i == 0:
+            grads(wrap(me + FAR), 0)
+        else:
+            grads(toward(0, FAR - i), 0)
+            grads(toward(1, FAR - i), 1)
 
     def block_sum(b):
         a = jnp.zeros((BLK, DH), F32)
@@ -288,125 +286,101 @@
         dk_ref[b] = (a * SCALE).astype(BF16)
         dv_ref[b] = g.astype(BF16)
 
-    def query_work(t, bias, h):
-        for D in range(2):
-            if is_int(t) and D == 1 and t > 7:
-                continue
-            c = from_behind(D, t)
-            if h == 0:
-                bias[D] = stage(c, D)
-            scores(c, D, h, bias[D])
-            if h == HEADS - 1:
-                to_candidate(st_out, st_in, st_s, st_r, c, me).start()
-
-    def grad_work(t, h):
-        for D in range(2):
-            if is_int(t) and D == 0 and t > 7:
-                continue
-            c = from_behind(D, t)
-            weights_grad(c, h)
-            if h == HEADS - 1:
-                to_candidate(del_out, del_in, de_s, de_r, c, me).start()
-
-    def gather_slot(s, extra=lambda h: None):
-        bias = {}
-        for h in range(HEADS):
-            if not is_int(s) or s <= 8:
-                gather_head(0, s, h)
-            if not is_int(s) or s > LAG:
-                gather_head(1, s - LAG, h)
-            elif s == LAG:
-                gather_first(1, h)
-            if not is_int(s) or s <= 8:
-                query_work(s, bias, h)
-            if not is_int(s) or s > LAG:
-                grad_work(s - LAG, h)
-            extra(h)
-
-    for h in range(HEADS):
-        gather_first(0, h)
+    def query_step(t):
+        gather_step(0, t)
+        for c, D in behind(t):
+            bias = stage(c, D)
+            for h in range(HEADS):
+                scores(c, D, h, bias)
+        for c, D in behind(t):
+            to_candidate(st_out, st_in, st_s, st_r, c, me).start()
+
+    def grad_step(t):
+        gather_step(1, t)
+        for c, D in behind(t):
+            for h in range(HEADS):
+                weights_grad(c, h)
+        for c, D in behind(t):
+            to_candidate(del_out, del_in, de_s, de_r, c, me).start()
+
+    def gather_slot(s):
+        query_step(s)
+        grad_step(s - LAG)
+
+    gather_first(0)
     own_scores()
     bias_me = stage(me, 0)
     for h in range(HEADS):
         scores(me, 0, h, bias_me)
-    for s in range(1, LAG + 1):
-        gather_slot(s)
-    loop(LAG + 1, 7, gather_slot)
-
-    def own_too(h):
+    query_step(1)
+    gather_first(1)
+    query_step(2)
+    loop(3, 7, gather_slot)
+    gather_slot(7)
+    gather_slot(8)
+    for h in range(HEADS):
         weights_grad(me, h)
         own_weights_grad(h)
-
     dks[EMPTY] = jnp.zeros((BLK, DH), F32)
     dvs[EMPTY] = jnp.zeros((BLK, DH), F32)
-    gather_slot(7)
-    gather_slot(8)
-    for s in range(9, 8 + LAG):
-        gather_slot(s, own_too if s == 9 else lambda h: None)
+    grad_step(7)
     combine_logsum()
-    gather_slot(8 + LAG)
+    grad_step(8)
     each_peer(lambda p: to_holder(lse_all, ls_s, ls_r, wrap(me + p), p).wait_recv())
-
-    for h in range(HEADS):
-        chain_head(0, 0, h)
-    for t in range(1, 5):
+    fac[:, :HEADS, :] = jnp.exp(st_out[:, :HEADS, :] - lse_all[:, :HEADS, :])
+
+    chain_step(0, 0)
+    for t in range(1, 9):
         gather_sent(0, t)
-    for h in range(HEADS):
-        chain_head(0, 1, h)
-    for t in range(5, 9):
-        gather_sent(0, t)
+    chain_step(0, 1)
     combine_deltas()
-    for h in range(HEADS):
-        chain_head(0, 2, h)
+    chain_step(0, 2)
     each_peer(lambda p: to_holder(delta_all, dl_s, dl_r, wrap(me + p), p).wait_recv())
-    for h in range(HEADS):
-        chain_grads(0, h)
-        chain_head(1, 0, h)
-    for h in range(HEADS):
-        chain_grads(1, h)
+    chain_grads(0)
+    chain_step(1, 0)
+    chain_grads(1)
 
     def chain_slot(u):
-        for h in range(HEADS):
-            if not is_int(u) or u < 8:
-                chain_head(0, u, h)
-            chain_head(1, u - 2, h)
-            chain_grads(u - 1, h)
-
-    loop(3, 5, chain_slot)
-    chain_slot(5)
+        chain_step(0, u)
+        chain_step(1, u - LAG)
+        chain_grads(u - 1)
+
+    chain_slot(3)
+    grads(me, 0)
+    loop(4, 6, chain_slot)
     for t in range(1, 9):
         gather_sent(1, t)
     chain_slot(6)
+    own_grads()
+    chain_slot(7)
+    chain_grads(7)
+    chain_step(1, 6)
+    for h in range(HEADS):
+        x = own_ou[h] * own_factor(h) + ou[me, h] * fac[me, h : h + 1, :]
+        for D in range(2):
+            if h % 2 == 0:
+                chain_copy(0, D, 1, h // 2).wait_recv()
+            x = x + rf[0, D, 0, h]
+        att_ref[:, head(h)] = x.T.astype(BF16)
+    loop(0, CB_DEV // 2, block_sum)
+    chain_step(1, 7)
+    loop(CB_DEV // 2, CB_DEV, block_sum)
     each_peer(lambda p: to_candidate(st_out, st_in, st_s, st_r, wrap(me + p), me).wait_send())
     each_peer(lambda p: to_holder(lse_all, ls_s, ls_r, me, p).wait_send())
-    chain_slot(7)
     each_peer(lambda p: to_candidate(del_out, del_in, de_s, de_r, wrap(me + p), me).wait_send())
     each_peer(lambda p: to_holder(delta_all, dl_s, dl_r, me, p).wait_send())
-    for h in range(HEADS):
-        chain_head(1, 6, h)
-        chain_grads(7, h)
-        grads(me, 0, h)
-        own_grads(h)
-    for h in range(HEADS):
-        x = own_ou[h] * own_factor(h) + ou[me, h] * factor(me, h)
-        for D in range(2):
-            chain_copy(0, D, 1, h).wait_recv()
-            x = x + rf[0, D, 0, h]
-        att_ref[:, head(h)] = x.T.astype(BF16)
-        chain_head(1, 7, h)
-    loop(0, CB_DEV, block_sum)
     for i in range(8):
         chain_sent(0, i)
-    for i in range(6):
+    for i in range(7):
         chain_sent(1, i)
     for h in range(HEADS):
         x = own_qu[h] + qu[me, h]
         for D in range(2):
-            chain_copy(1, D, 1, h).wait_recv()
+            if h % 2 == 0:
+                chain_copy(1, D, 1, h // 2).wait_recv()
             x = x + rf[1, D, 0, h]
         qg_ref[:, head(h)] = (x * SCALE).T.astype(BF16)
-    for i in range(6, 8):
-        chain_sent(1, i)
+    chain_sent(1, 7)
 
 
 def ring(ids, q, k, v, ok, ov, g):
@@ -432,13 +406,13 @@
             V((N,) + tile, F32), V((N,) + tile, F32),
             V(tile, F32), V(tile, F32), V(tile, F32), V(tile, F32),
             V((8, 128), F32), V((8, 128), F32),
-            stats, stats, stats, stats, stats, stats,
+            stats, stats, stats, stats, stats, stats, stats,
             V((3, KEYS, ROWS), BF16), V((3, KEYS, ROWS), BF16), V((2, DH, KEYS), BF16),
             V((2 * N + 1, BLK, DH), F32), V((2 * N + 1, BLK, DH), F32),
             pltpu.SMEM((N, 2), jnp.int32),
             V((2, 2, FAR - WIDE) + tile, BF16), V((2, 2, FAR - WIDE) + tile, BF16),
             V((2, 2, WIDE) + tile, F32), V((2, 2, WIDE) + tile, F32),
-            D((2, 2, 8, HEADS)), D((2, 2, 8, HEADS)), D((2, 2, 8, HEADS)), D((2, 2, 8, HEADS)),
+            D((2, 2, FAR, 2)), D((2, 2, FAR, 2)), D((2, 2, FAR, 2)), D((2, 2, FAR, 2)),
             D((N,)), D((N,)), D((N,)), D((N,)), D((N,)), D((N,)), D((N,)), D((N,)),
         ],
         compiler_params=pltpu.CompilerParams(

time: 148 us -> 144 us (0.973)
  Pallas kernels: 147 us -> 143 us
    pallas_call x1, Pallas kernels: 144 us -> 141 us  [ring(): pl.pallas_call(ring_kernel, in_specs=[pl.BlockSpec(memory_space=pltpu.SME...]
where the time goes in v4:
time: 144 us
  Pallas kernels  143 us (99%)
    pallas_call x1, Pallas kernels, ring(): pl.pallas_call(ring_kernel, in_specs=[pl.BlockSpec(memory_space=pltpu.SME...  141 us

profile of v4, /device:TPU:6, one launch (start us, length us, event | category | flops | bytes accessed | tf_op | source)
XLA Modules:
  0.0 143.6 jit_solution(193160776654489385)
XLA Ops:
  0.6 140.5 %ring_attention.1 = (bf16[128,512]{1,0:T(8,128)(2,1)}, bf16[128,512]{1,0:T(8,128)(2,1)}, bf16[128,128]{1,0:T(8,128)(2,1)}, bf16[128,128]{1,0:T(8,128)(2,1)}, bf1...) custom-call(s32[16,24]{1,0:T(8,128)} %ids_ref.1, bf16[128,512]{1,0:T(8,128)(2,1)} %q_ref.1, ...), custom_call_target="tpu_custom_call" | custom-call | tf_op jit(solution)/shard_map/ring_attention/pallas_call | solution.py:393
  141.2 2.5 %hand_on.1 = (bf16[128,512]{1,0:T(8,128)(2,1)}, bf16[128,512]{1,0:T(8,128)(2,1)}, bf16[128,128]{1,0:T(8,128)(2,1)}, bf16[128,128]{1,0:T(8,128)(2,1)}, bf16[16,12...) custom-call(bf16[128,512]{1,0:T(8,128)(2,1)} %get-tuple-element.18.refs_0_, ...), custom_call_target="tpu_custom_call" | custom-call | tf_op jit(solution)/shard_map/hand_on/pallas_call | solution.py:433

commit v5 on v4

--- a/solution.py
+++ b/solution.py
@@ -18,10 +18,10 @@
 EMPTY = 2 * N
 SCALE = 1.0 / math.sqrt(DH)
 HIDDEN = -1e30
-FLOOR = -1e25
+FLOOR = -(2.0**83)
 WIDE = 2
 FAR = 8
-LAG = 2
+MARK = 256
 F32 = jnp.float32
 BF16 = jnp.bfloat16
 NT = (((1,), (1,)), ((), ()))
@@ -49,9 +49,9 @@
     att_ref, qg_ref, okg_ref, ovg_ref, dk_ref, dv_ref,
     q_all, g_all, nk, nv, lw, dp, ou, qu,
     own_lw, own_dp, own_ou, own_qu, own_st, own_del,
-    st_out, st_in, del_out, del_in, lse_all, delta_all, fac,
+    st_out, st_in, lse_all, fac,
     ds_t, p_t, tr, dks, dvs, sel, sb, rb, sf, rf,
-    g_send, g_recv, c_send, c_recv, st_s, st_r, de_s, de_r, ls_s, ls_r, dl_s, dl_r,
+    g_send, g_recv, c_send, c_recv, st_s, st_r, ls_s, ls_r,
 ):
     me = lax.axis_index("ctx")
     low = me * CB_DEV
@@ -165,14 +165,14 @@
         d = dot(nv[c], g_all[c, h], NT)
         dp[c, h] = d
         e = lw[c, h].astype(BF16).astype(F32)
-        del_out[c, h : h + 1, :] = jnp.sum(e * d, axis=0, keepdims=True)
+        st_out[c, 2 * HEADS + h : 2 * HEADS + h + 1, :] = jnp.sum(e * d, axis=0, keepdims=True)
 
     def grads(c, D):
         tr[D] = nk[c].T
         for h in range(HEADS):
             w = lw[c, h] * fac[c, h : h + 1, :]
             p_t[D, :, head(h)] = w.astype(BF16)
-            ds = (w * (dp[c, h] - delta_all[c, h : h + 1, :])).astype(BF16)
+            ds = (w * (dp[c, h] - lse_all[c, HEADS + h : HEADS + h + 1, :])).astype(BF16)
             ds_t[D, :, head(h)] = ds
             qu[c, h] = dot(tr[D], ds)
         a = dot(ds_t[D], q_all[c].reshape(ROWS, DH))
@@ -209,31 +209,26 @@
         for h in range(HEADS):
             w = own_lw[h] * own_factor(h)
             p_t[2, :BLK, head(h)] = w.astype(BF16)
-            ds = (w * (own_dp[h] - delta_all[me, h : h + 1, :])).astype(BF16)
+            ds = (w * (own_dp[h] - lse_all[me, HEADS + h : HEADS + h + 1, :])).astype(BF16)
             ds_t[2, :BLK, head(h)] = ds
             own_qu[h] = dot(kt, ds)
         okg_ref[...] = (dot(ds_t[2, :BLK, :], q_all[me].reshape(ROWS, DH)) * SCALE).astype(BF16)
         ovg_ref[...] = dot(p_t[2, :BLK, :], g_all[me].reshape(ROWS, DH)).astype(BF16)
 
-    def combine_logsum():
+    def combine():
         st_in[me] = st_out[me]
         each_peer(lambda p: to_candidate(st_out, st_in, st_s, st_r, wrap(me + p), wrap(me + p)).wait_recv())
         maxima = st_in[:, :HEADS, :]
-        totals = st_in[:, HEADS:, :]
+        totals = st_in[:, HEADS : 2 * HEADS, :]
+        parts = st_in[:, 2 * HEADS : 3 * HEADS, :]
         own_max = own_st[:HEADS, :]
         top = jnp.maximum(jnp.max(maxima, axis=0), own_max)
-        total = own_st[HEADS:, :] * jnp.exp(own_max - top) + jnp.sum(totals * jnp.exp(maxima - top[None]), axis=0)
+        lift = jnp.exp(maxima - top[None])
+        own_lift = jnp.exp(own_max - top)
+        total = own_st[HEADS:, :] * own_lift + jnp.sum(totals * lift, axis=0)
         lse_all[me, :HEADS, :] = top + jnp.log(total)
+        lse_all[me, HEADS:, :] = (own_del[:HEADS, :] * own_lift + jnp.sum(parts * lift, axis=0)) / total
         each_peer(lambda p: to_holder(lse_all, ls_s, ls_r, me, p).start())
-
-    def combine_deltas():
-        del_in[me] = del_out[me]
-        each_peer(lambda p: to_candidate(del_out, del_in, de_s, de_r, wrap(me + p), wrap(me + p)).wait_recv())
-        logsum = lse_all[me, :HEADS, :]
-        total = own_del[:HEADS, :] * jnp.exp(own_st[:HEADS, :] - logsum)
-        total = total + jnp.sum(del_in[:, :HEADS, :] * jnp.exp(st_in[:, :HEADS, :] - logsum[None]), axis=0)
-        delta_all[me, :HEADS, :] = total
-        each_peer(lambda p: to_holder(delta_all, dl_s, dl_r, me, p).start())
 
     def buffers(chain, D, d):
         if is_int(d) and d <= WIDE:
@@ -242,8 +237,9 @@
 
     def chain_copy(chain, D, d, b):
         src, dst = buffers(chain, D, d)
+        rows = pl.ds(0, MARK + 16 if chain == 0 else MARK)
         return pltpu.make_async_remote_copy(
-            src_ref=src.at[pl.ds(2 * b, 2)], dst_ref=dst.at[pl.ds(2 * b, 2)],
+            src_ref=src.at[b, rows], dst_ref=dst.at[b, rows],
             send_sem=c_send.at[chain, D, d - 1, b], recv_sem=c_recv.at[chain, D, d - 1, b],
             device_id={"ctx": nbr[D]},
         )
@@ -256,11 +252,29 @@
             for D in ways(d, b):
                 c = toward(D, d)
                 out = buffers(chain, D, d)[0]
-                for h in (2 * b, 2 * b + 1):
-                    x = ou[c, h] * fac[c, h : h + 1, :] if chain == 0 else qu[c, h]
-                    if D in ways(d + 1, b):
-                        x = x + buffers(chain, D, d + 1)[1][h].astype(F32)
-                    out[h] = x.astype(out.dtype)
+                came = D in ways(d + 1, b)
+                arrived = buffers(chain, D, d + 1)[1] if came else None
+                if chain == 0 and came:
+                    old = arrived[b, MARK:, :].astype(F32)
+                marks = []
+                for j in range(2):
+                    h = 2 * b + j
+                    if chain == 0:
+                        m = st_out[c, h : h + 1, :]
+                        r = jnp.ceil(m * 0.25) * 4.0
+                        if came:
+                            r = jnp.maximum(r, old[8 * j : 8 * j + 1])
+                        x = ou[c, h] * jnp.exp(m - r)
+                        if came:
+                            x = x + arrived[b, head(j), :].astype(F32) * jnp.exp(old[8 * j : 8 * j + 1] - r)
+                        marks.append(jnp.broadcast_to(r, (8, 128)))
+                    else:
+                        x = qu[c, h]
+                        if came:
+                            x = x + arrived[b, head(j), :].astype(F32)
+                    out[b, head(j), :] = x.astype(out.dtype)
+                if chain == 0:
+                    out[b, MARK:, :] = jnp.concatenate(marks, axis=0).astype(out.dtype)
             for D in ways(d, b):
                 chain_copy(chain, D, d, b).start()
 
@@ -292,8 +306,6 @@
             bias = stage(c, D)
             for h in range(HEADS):
                 scores(c, D, h, bias)
-        for c, D in behind(t):
-            to_candidate(st_out, st_in, st_s, st_r, c, me).start()
 
     def grad_step(t):
         gather_step(1, t)
@@ -301,74 +313,71 @@
             for h in range(HEADS):
                 weights_grad(c, h)
         for c, D in behind(t):
-            to_candidate(del_out, del_in, de_s, de_r, c, me).start()
+            to_candidate(st_out, st_in, st_s, st_r, c, me).start()
 
     def gather_slot(s):
         query_step(s)
-        grad_step(s - LAG)
+        grad_step(s - 1)
 
     gather_first(0)
+    gather_first(1)
     own_scores()
     bias_me = stage(me, 0)
     for h in range(HEADS):
         scores(me, 0, h, bias_me)
     query_step(1)
-    gather_first(1)
-    query_step(2)
-    loop(3, 7, gather_slot)
+    loop(2, 7, gather_slot)
     gather_slot(7)
     gather_slot(8)
+
+    chain_step(0, 0)
+    grad_step(8)
     for h in range(HEADS):
         weights_grad(me, h)
         own_weights_grad(h)
     dks[EMPTY] = jnp.zeros((BLK, DH), F32)
     dvs[EMPTY] = jnp.zeros((BLK, DH), F32)
-    grad_step(7)
-    combine_logsum()
-    grad_step(8)
+    chain_step(0, 1)
+    for t in range(1, 9):
+        gather_sent(0, t)
+    chain_step(0, 2)
+    combine()
+    chain_step(0, 3)
+    for t in range(1, 9):
+        gather_sent(1, t)
+    chain_step(0, 4)
     each_peer(lambda p: to_holder(lse_all, ls_s, ls_r, wrap(me + p), p).wait_recv())
     fac[:, :HEADS, :] = jnp.exp(st_out[:, :HEADS, :] - lse_all[:, :HEADS, :])
 
-    chain_step(0, 0)
-    for t in range(1, 9):
-        gather_sent(0, t)
-    chain_step(0, 1)
-    combine_deltas()
-    chain_step(0, 2)
-    each_peer(lambda p: to_holder(delta_all, dl_s, dl_r, wrap(me + p), p).wait_recv())
     chain_grads(0)
     chain_step(1, 0)
     chain_grads(1)
-
-    def chain_slot(u):
-        chain_step(0, u)
-        chain_step(1, u - LAG)
-        chain_grads(u - 1)
-
-    chain_slot(3)
+    for i in range(1, 4):
+        chain_step(0, i + 4)
+        chain_step(1, i)
+        chain_grads(i + 1)
     grads(me, 0)
-    loop(4, 6, chain_slot)
-    for t in range(1, 9):
-        gather_sent(1, t)
-    chain_slot(6)
+    chain_step(1, 4)
+    chain_grads(5)
     own_grads()
-    chain_slot(7)
-    chain_grads(7)
-    chain_step(1, 6)
     for h in range(HEADS):
         x = own_ou[h] * own_factor(h) + ou[me, h] * fac[me, h : h + 1, :]
         for D in range(2):
-            if h % 2 == 0:
-                chain_copy(0, D, 1, h // 2).wait_recv()
-            x = x + rf[0, D, 0, h]
+            b, j = h // 2, h % 2
+            if j == 0:
+                chain_copy(0, D, 1, b).wait_recv()
+            lift = jnp.exp(rf[0, D, 0, b, MARK + 8 * j : MARK + 8 * j + 1, :] - lse_all[me, h : h + 1, :])
+            x = x + rf[0, D, 0, b, head(j), :] * lift
         att_ref[:, head(h)] = x.T.astype(BF16)
+    chain_step(1, 5)
+    chain_grads(6)
+    chain_grads(7)
+    chain_step(1, 6)
     loop(0, CB_DEV // 2, block_sum)
     chain_step(1, 7)
     loop(CB_DEV // 2, CB_DEV, block_sum)
     each_peer(lambda p: to_candidate(st_out, st_in, st_s, st_r, wrap(me + p), me).wait_send())
     each_peer(lambda p: to_holder(lse_all, ls_s, ls_r, me, p).wait_send())
-    each_peer(lambda p: to_candidate(del_out, del_in, de_s, de_r, wrap(me + p), me).wait_send())
-    each_peer(lambda p: to_holder(delta_all, dl_s, dl_r, me, p).wait_send())
     for i in range(8):
         chain_sent(0, i)
     for i in range(7):
@@ -376,9 +385,10 @@
     for h in range(HEADS):
         x = own_qu[h] + qu[me, h]
         for D in range(2):
-            if h % 2 == 0:
-                chain_copy(1, D, 1, h // 2).wait_recv()
-            x = x + rf[1, D, 0, h]
+            b, j = h // 2, h % 2
+            if j == 0:
+                chain_copy(1, D, 1, b).wait_recv()
+            x = x + rf[1, D, 0, b, head(j), :]
         qg_ref[:, head(h)] = (x * SCALE).T.astype(BF16)
     chain_sent(1, 7)
 
@@ -388,7 +398,7 @@
     shape = jax.ShapeDtypeStruct
     V = pltpu.VMEM
     D = pltpu.SemaphoreType.DMA
-    stats = V((N, 8, 128), F32)
+    message = (2, MARK + 16, 128)
     tile = (HEADS, 128, 128)
     return pl.pallas_call(
         ring_kernel,
@@ -406,14 +416,14 @@
             V((N,) + tile, F32), V((N,) + tile, F32),
             V(tile, F32), V(tile, F32), V(tile, F32), V(tile, F32),
             V((8, 128), F32), V((8, 128), F32),
-            stats, stats, stats, stats, stats, stats, stats,
+            V((N, 16, 128), F32), V((N, 16, 128), F32), V((N, 8, 128), F32), V((N, 8, 128), F32),
             V((3, KEYS, ROWS), BF16), V((3, KEYS, ROWS), BF16), V((2, DH, KEYS), BF16),
             V((2 * N + 1, BLK, DH), F32), V((2 * N + 1, BLK, DH), F32),
             pltpu.SMEM((N, 2), jnp.int32),
-            V((2, 2, FAR - WIDE) + tile, BF16), V((2, 2, FAR - WIDE) + tile, BF16),
-            V((2, 2, WIDE) + tile, F32), V((2, 2, WIDE) + tile, F32),
+            V((2, 2, FAR - WIDE) + message, BF16), V((2, 2, FAR - WIDE) + message, BF16),
+            V((2, 2, WIDE) + message, F32), V((2, 2, WIDE) + message, F32),
             D((2, 2, FAR, 2)), D((2, 2, FAR, 2)), D((2, 2, FAR, 2)), D((2, 2, FAR, 2)),
-            D((N,)), D((N,)), D((N,)), D((N,)), D((N,)), D((N,)), D((N,)), D((N,)),
+            D((N,)), D((N,)), D((N,)), D((N,)),
         ],
         compiler_params=pltpu.CompilerParams(
             collective_id=0, has_side_effects=True, vmem_limit_bytes=60 * 1024 * 1024

time: 144 us -> 140 us (0.972)
  Pallas kernels: 143 us -> 140 us
    pallas_call x1, Pallas kernels: 141 us -> 137 us  [ring(): pl.pallas_call(ring_kernel, in_specs=[pl.BlockSpec(memory_space=pltpu.SME...]
where the time goes in v5:
time: 140 us
  Pallas kernels  140 us (100%)
    pallas_call x1, Pallas kernels, ring(): pl.pallas_call(ring_kernel, in_specs=[pl.BlockSpec(memory_space=pltpu.SME...  137 us

profile of v5, /device:TPU:6, one launch (start us, length us, event | category | flops | bytes accessed | tf_op | source)
XLA Modules:
  0.0 140.2 jit_solution(6404087413319709081)
XLA Ops:
  0.6 137.1 %ring_attention.1 = (bf16[128,512]{1,0:T(8,128)(2,1)}, bf16[128,512]{1,0:T(8,128)(2,1)}, bf16[128,128]{1,0:T(8,128)(2,1)}, bf16[128,128]{1,0:T(8,128)(2,1)}, bf1...) custom-call(s32[16,24]{1,0:T(8,128)} %ids_ref.1, bf16[128,512]{1,0:T(8,128)(2,1)} %q_ref.1, ...), custom_call_target="tpu_custom_call" | custom-call | tf_op jit(solution)/shard_map/ring_attention/pallas_call | solution.py:403
  137.7 2.5 %hand_on.1 = (bf16[128,512]{1,0:T(8,128)(2,1)}, bf16[128,512]{1,0:T(8,128)(2,1)}, bf16[128,128]{1,0:T(8,128)(2,1)}, bf16[128,128]{1,0:T(8,128)(2,1)}, bf16[16,12...) custom-call(bf16[128,512]{1,0:T(8,128)(2,1)} %get-tuple-element.18.refs_0_, ...), custom_call_target="tpu_custom_call" | custom-call | tf_op jit(solution)/shard_map/hand_on/pallas_call | solution.py:443

commit v6 on v5

--- a/solution.py
+++ b/solution.py
@@ -19,7 +19,7 @@
 SCALE = 1.0 / math.sqrt(DH)
 HIDDEN = -1e30
 FLOOR = -(2.0**83)
-WIDE = 2
+NEAR = 2
 FAR = 8
 MARK = 256
 F32 = jnp.float32
@@ -50,8 +50,9 @@
     q_all, g_all, nk, nv, lw, dp, ou, qu,
     own_lw, own_dp, own_ou, own_qu, own_st, own_del,
     st_out, st_in, lse_all, fac,
-    ds_t, p_t, tr, dks, dvs, sel, sb, rb, sf, rf,
-    g_send, g_recv, c_send, c_recv, st_s, st_r, ls_s, ls_r,
+    ds_t, p_t, tr, dks, dvs, sel, sb, rb,
+    fk, fv, f_lw, f_dp, f_ou, f_max,
+    g_send, g_recv, c_send, c_recv, st_s, st_r, ls_s, ls_r, f_send, f_recv,
 ):
     me = lax.axis_index("ctx")
     low = me * CB_DEV
@@ -126,7 +127,13 @@
             device_id={"ctx": wrap(me + p)},
         )
 
-    def stage(c, D):
+    def biases(count):
+        return (
+            jnp.where(count >= 1, 0.0, HIDDEN).astype(F32),
+            jnp.where(count >= 2, 0.0, HIDDEN).astype(F32),
+        )
+
+    def pick(c, low):
         first = jnp.int32(CB_DEV)
         last = jnp.int32(-1)
         count = jnp.int32(0)
@@ -136,6 +143,10 @@
             first = jnp.where(inside, jnp.minimum(first, b), first)
             last = jnp.where(inside, jnp.maximum(last, b), last)
             count = count + jnp.where(inside, 1, 0)
+        return first, last, count
+
+    def stage(c):
+        first, last, count = pick(c, low)
         sel[c, 0] = jnp.where(count >= 1, first, -1)
         sel[c, 1] = jnp.where(count >= 2, last, -1)
         first = jnp.minimum(first, CB_DEV - 1)
@@ -144,18 +155,24 @@
         nk[c, BLK:, :] = k_ref[last]
         nv[c, :BLK, :] = v_ref[first]
         nv[c, BLK:, :] = v_ref[last]
+
+    def score_bias(c, D):
         tr[D] = nv[c].T
-        bias0 = jnp.where(count >= 1, 0.0, HIDDEN).astype(F32)
-        bias1 = jnp.where(count >= 2, 0.0, HIDDEN).astype(F32)
-        return bias0, bias1
-
-    def scores(c, D, h, bias):
-        s = dot(nk[c], q_all[c, h], NT) * SCALE
+        return (
+            jnp.where(sel[c, 0] >= 0, 0.0, HIDDEN).astype(F32),
+            jnp.where(sel[c, 1] >= 0, 0.0, HIDDEN).astype(F32),
+        )
+
+    def local_scores(keys, q, bias):
+        s = dot(keys, q, NT) * SCALE
         s0 = s[:BLK] + bias[0]
         s1 = s[BLK:] + bias[1]
         m = jnp.max(jnp.maximum(s0, s1), axis=0, keepdims=True)
         m = jnp.maximum(m, FLOOR)
-        e = jnp.exp(jnp.concatenate([s0, s1], axis=0) - m)
+        return m, jnp.exp(jnp.concatenate([s0, s1], axis=0) - m)
+
+    def scores(c, D, h, bias):
+        m, e = local_scores(nk[c], q_all[c, h], bias)
         lw[c, h] = e
         st_out[c, h : h + 1, :] = m
         st_out[c, HEADS + h : HEADS + h + 1, :] = jnp.sum(e, axis=0, keepdims=True)
@@ -167,14 +184,16 @@
         e = lw[c, h].astype(BF16).astype(F32)
         st_out[c, 2 * HEADS + h : 2 * HEADS + h + 1, :] = jnp.sum(e * d, axis=0, keepdims=True)
 
-    def grads(c, D):
-        tr[D] = nk[c].T
+    def grads(c, D, back=True):
+        if back:
+            tr[D] = nk[c].T
         for h in range(HEADS):
             w = lw[c, h] * fac[c, h : h + 1, :]
             p_t[D, :, head(h)] = w.astype(BF16)
             ds = (w * (dp[c, h] - lse_all[c, HEADS + h : HEADS + h + 1, :])).astype(BF16)
             ds_t[D, :, head(h)] = ds
-            qu[c, h] = dot(tr[D], ds)
+            if back:
+                qu[c, h] = dot(tr[D], ds)
         a = dot(ds_t[D], q_all[c].reshape(ROWS, DH))
         b = dot(p_t[D], g_all[c].reshape(ROWS, DH))
         for slot in range(2):
@@ -214,6 +233,35 @@
             own_qu[h] = dot(kt, ds)
         okg_ref[...] = (dot(ds_t[2, :BLK, :], q_all[me].reshape(ROWS, DH)) * SCALE).astype(BF16)
         ovg_ref[...] = dot(p_t[2, :BLK, :], g_all[me].reshape(ROWS, DH)).astype(BF16)
+
+    def near_copy(D, d, w):
+        return pltpu.make_async_remote_copy(
+            src_ref=(nk, nv)[w].at[toward(D, d)], dst_ref=(fk, fv)[w].at[2 * D + d - 1],
+            send_sem=f_send.at[D, d - 1, w], recv_sem=f_recv.at[D, d - 1, w],
+            device_id={"ctx": toward(D, d)},
+        )
+
+    def near_scores(D, d):
+        n = 2 * D + d - 1
+        for w in range(2):
+            near_copy(D, d, w).wait_recv()
+        count = pick(me, from_behind(D, d) * CB_DEV)[2]
+        bias = biases(count)
+        tr[D] = fv[n].T
+        for h in range(HEADS):
+            m, e = local_scores(fk[n], q_all[me, h], bias)
+            f_lw[n, h] = e
+            f_max[n, h : h + 1, :] = m
+            f_ou[n, h] = dot(tr[D], e.astype(BF16))
+            f_dp[n, h] = dot(fv[n], g_all[me, h], NT)
+
+    def near_grads(D, d):
+        n = 2 * D + d - 1
+        tr[D] = fk[n].T
+        for h in range(HEADS):
+            w = f_lw[n, h] * jnp.exp(f_max[n, h : h + 1, :] - lse_all[me, h : h + 1, :])
+            ds = (w * (f_dp[n, h] - lse_all[me, HEADS + h : HEADS + h + 1, :])).astype(BF16)
+            own_qu[h] += dot(tr[D], ds)
 
     def combine():
         st_in[me] = st_out[me]
@@ -231,9 +279,7 @@
         each_peer(lambda p: to_holder(lse_all, ls_s, ls_r, me, p).start())
 
     def buffers(chain, D, d):
-        if is_int(d) and d <= WIDE:
-            return sf.at[chain, D, d - 1], rf.at[chain, D, d - 1]
-        return sb.at[chain, D, d - 1 - WIDE], rb.at[chain, D, d - 1 - WIDE]
+        return sb.at[chain, D, d - 1 - NEAR], rb.at[chain, D, d - 1 - NEAR]
 
     def chain_copy(chain, D, d, b):
         src, dst = buffers(chain, D, d)
@@ -241,7 +287,7 @@
         return pltpu.make_async_remote_copy(
             src_ref=src.at[b, rows], dst_ref=dst.at[b, rows],
             send_sem=c_send.at[chain, D, d - 1, b], recv_sem=c_recv.at[chain, D, d - 1, b],
-            device_id={"ctx": nbr[D]},
+            device_id={"ctx": toward(D, NEAR + 1) if d == NEAR + 1 else nbr[D]},
         )
 
     def chain_step(chain, i):
@@ -303,7 +349,9 @@
     def query_step(t):
         gather_step(0, t)
         for c, D in behind(t):
-            bias = stage(c, D)
+            if not is_int(t) or t > NEAR:
+                stage(c)
+            bias = score_bias(c, D)
             for h in range(HEADS):
                 scores(c, D, h, bias)
 
@@ -321,12 +369,19 @@
 
     gather_first(0)
     gather_first(1)
+    for d in range(1, NEAR + 1):
+        for D in range(2):
+            stage(toward(D, d))
+            for w in range(2):
+                near_copy(D, d, w).start()
     own_scores()
-    bias_me = stage(me, 0)
+    stage(me)
+    bias_me = score_bias(me, 0)
     for h in range(HEADS):
         scores(me, 0, h, bias_me)
     query_step(1)
-    loop(2, 7, gather_slot)
+    gather_slot(2)
+    loop(3, 7, gather_slot)
     gather_slot(7)
     gather_slot(8)
 
@@ -338,11 +393,15 @@
     dks[EMPTY] = jnp.zeros((BLK, DH), F32)
     dvs[EMPTY] = jnp.zeros((BLK, DH), F32)
     chain_step(0, 1)
+    near_scores(0, 1)
+    near_scores(1, 1)
     for t in range(1, 9):
         gather_sent(0, t)
     chain_step(0, 2)
     combine()
     chain_step(0, 3)
+    near_scores(0, 2)
+    near_scores(1, 2)
     for t in range(1, 9):
         gather_sent(1, t)
     chain_step(0, 4)
@@ -352,45 +411,59 @@
     chain_grads(0)
     chain_step(1, 0)
     chain_grads(1)
-    for i in range(1, 4):
-        chain_step(0, i + 4)
-        chain_step(1, i)
-        chain_grads(i + 1)
-    grads(me, 0)
+    chain_step(0, 5)
+    chain_step(1, 1)
+    chain_grads(2)
+    for D in range(2):
+        grads(toward(D, 2), D, False)
+    chain_step(1, 2)
+    chain_grads(3)
+    for D in range(2):
+        grads(toward(D, 1), D, False)
+    chain_step(1, 3)
+    chain_grads(4)
+    own_grads()
+    near_grads(0, 1)
+    near_grads(1, 1)
     chain_step(1, 4)
     chain_grads(5)
-    own_grads()
+    chain_step(1, 5)
+    grads(me, 0)
+    near_grads(0, 2)
+    near_grads(1, 2)
+    last = NEAR + 1
     for h in range(HEADS):
+        b, j = h // 2, h % 2
         x = own_ou[h] * own_factor(h) + ou[me, h] * fac[me, h : h + 1, :]
+        for n in range(2 * NEAR):
+            x = x + f_ou[n, h] * jnp.exp(f_max[n, h : h + 1, :] - lse_all[me, h : h + 1, :])
         for D in range(2):
-            b, j = h // 2, h % 2
             if j == 0:
-                chain_copy(0, D, 1, b).wait_recv()
-            lift = jnp.exp(rf[0, D, 0, b, MARK + 8 * j : MARK + 8 * j + 1, :] - lse_all[me, h : h + 1, :])
-            x = x + rf[0, D, 0, b, head(j), :] * lift
+                chain_copy(0, D, last, b).wait_recv()
+            came = buffers(0, D, last)[1]
+            r = came[b, MARK:, :].astype(F32)[8 * j : 8 * j + 1]
+            x = x + came[b, head(j), :].astype(F32) * jnp.exp(r - lse_all[me, h : h + 1, :])
         att_ref[:, head(h)] = x.T.astype(BF16)
-    chain_step(1, 5)
-    chain_grads(6)
-    chain_grads(7)
-    chain_step(1, 6)
-    loop(0, CB_DEV // 2, block_sum)
-    chain_step(1, 7)
-    loop(CB_DEV // 2, CB_DEV, block_sum)
+    loop(0, CB_DEV, block_sum)
     each_peer(lambda p: to_candidate(st_out, st_in, st_s, st_r, wrap(me + p), me).wait_send())
     each_peer(lambda p: to_holder(lse_all, ls_s, ls_r, me, p).wait_send())
-    for i in range(8):
+    for d in range(1, NEAR + 1):
+        for D in range(2):
+            for w in range(2):
+                near_copy(D, d, w).wait_send()
+    for i in range(6):
         chain_sent(0, i)
-    for i in range(7):
+    for i in range(5):
         chain_sent(1, i)
     for h in range(HEADS):
+        b, j = h // 2, h % 2
         x = own_qu[h] + qu[me, h]
         for D in range(2):
-            b, j = h // 2, h % 2
             if j == 0:
-                chain_copy(1, D, 1, b).wait_recv()
-            x = x + rf[1, D, 0, b, head(j), :]
+                chain_copy(1, D, last, b).wait_recv()
+            x = x + buffers(1, D, last)[1][b, head(j), :].astype(F32)
         qg_ref[:, head(h)] = (x * SCALE).T.astype(BF16)
-    chain_sent(1, 7)
+    chain_sent(1, 5)
 
 
 def ring(ids, q, k, v, ok, ov, g):
@@ -420,10 +493,12 @@
             V((3, KEYS, ROWS), BF16), V((3, KEYS, ROWS), BF16), V((2, DH, KEYS), BF16),
             V((2 * N + 1, BLK, DH), F32), V((2 * N + 1, BLK, DH), F32),
             pltpu.SMEM((N, 2), jnp.int32),
-            V((2, 2, FAR - WIDE) + message, BF16), V((2, 2, FAR - WIDE) + message, BF16),
-            V((2, 2, WIDE) + message, F32), V((2, 2, WIDE) + message, F32),
+            V((2, 2, FAR - NEAR) + message, BF16), V((2, 2, FAR - NEAR) + message, BF16),
+            V((2 * NEAR, KEYS, DH), BF16), V((2 * NEAR, KEYS, DH), BF16),
+            V((2 * NEAR, HEADS, KEYS, 128), F32), V((2 * NEAR, HEADS, KEYS, 128), F32),
+            V((2 * NEAR,) + tile, F32), V((2 * NEAR, 8, 128), F32),
             D((2, 2, FAR, 2)), D((2, 2, FAR, 2)), D((2, 2, FAR, 2)), D((2, 2, FAR, 2)),
-            D((N,)), D((N,)), D((N,)), D((N,)),
+            D((N,)), D((N,)), D((N,)), D((N,)), D((2, NEAR, 2)), D((2, NEAR, 2)),
         ],
         compiler_params=pltpu.CompilerParams(
             collective_id=0, has_side_effects=True, vmem_limit_bytes=60 * 1024 * 1024

time: 140 us -> 141 us (level); the launches traced: 140 us -> 138 us
  Pallas kernels: 140 us -> 137 us
    pallas_call x1, Pallas kernels: 137 us -> 135 us  [ring(): pl.pallas_call(ring_kernel, in_specs=[pl.BlockSpec(memory_space=pltpu.SME...]
where the time goes in v6:
time: 141 us; the launch traced here: 138 us
  Pallas kernels  137 us (97%)
    pallas_call x1, Pallas kernels, ring(): pl.pallas_call(ring_kernel, in_specs=[pl.BlockSpec(memory_space=pltpu.SME...  135 us

profile of v6, /device:TPU:6, one launch (start us, length us, event | category | flops | bytes accessed | tf_op | source)
XLA Modules:
  0.0 137.9 jit_solution(9585762238936320446)
XLA Ops:
  0.6 134.8 %ring_attention.1 = (bf16[128,512]{1,0:T(8,128)(2,1)}, bf16[128,512]{1,0:T(8,128)(2,1)}, bf16[128,128]{1,0:T(8,128)(2,1)}, bf16[128,128]{1,0:T(8,128)(2,1)}, bf1...) custom-call(s32[16,24]{1,0:T(8,128)} %ids_ref.1, bf16[128,512]{1,0:T(8,128)(2,1)} %q_ref.1, ...), custom_call_target="tpu_custom_call" | custom-call | tf_op jit(solution)/shard_map/ring_attention/pallas_call | solution.py:476
  135.5 2.5 %hand_on.1 = (bf16[128,512]{1,0:T(8,128)(2,1)}, bf16[128,512]{1,0:T(8,128)(2,1)}, bf16[128,128]{1,0:T(8,128)(2,1)}, bf16[128,128]{1,0:T(8,128)(2,1)}, bf16[16,12...) custom-call(bf16[128,512]{1,0:T(8,128)(2,1)} %get-tuple-element.18.refs_0_, ...), custom_call_target="tpu_custom_call" | custom-call | tf_op jit(solution)/shard_map/hand_on/pallas_call | solution.py:518

commit v7 on v6

--- a/solution.py
+++ b/solution.py
@@ -52,7 +52,7 @@
     st_out, st_in, lse_all, fac,
     ds_t, p_t, tr, dks, dvs, sel, sb, rb,
     fk, fv, f_lw, f_dp, f_ou, f_max,
-    g_send, g_recv, c_send, c_recv, st_s, st_r, ls_s, ls_r, f_send, f_recv,
+    g_send, g_recv, c_send, c_recv, st_s, st_r, ls_s, ls_r, f_send, f_recv, pace_sem,
 ):
     me = lax.axis_index("ctx")
     low = me * CB_DEV
@@ -70,11 +70,23 @@
     def each_peer(fn):
         loop(1, N, fn)
 
+    paired = lax.axis_size("head") % 2 == 0
+    side = lax.axis_index("head")
+    other = side + 1 - 2 * lax.rem(side, 2)
+
+    def pace(wait=True):
+        if paired:
+            pl.semaphore_signal(pace_sem, inc=1, device_id={"head": other})
+            if wait:
+                pl.semaphore_wait(pace_sem, 1)
+
     each_peer(lambda p: pl.semaphore_signal(barrier, inc=1, device_id={"ctx": wrap(me + p)}))
+    if paired:
+        pl.semaphore_signal(barrier, inc=1, device_id={"head": other})
     for h in range(HEADS):
         q_all[me, h] = q_ref[:, head(h)]
         g_all[me, h] = g_ref[:, head(h)]
-    pl.semaphore_wait(barrier, N - 1)
+    pl.semaphore_wait(barrier, N if paired else N - 1)
 
     def gather_copy(stream, D, t, b, c):
         part = (q_all, g_all)[stream].at[c, pl.ds(2 * b, 2)]
@@ -276,7 +288,13 @@
         total = own_st[HEADS:, :] * own_lift + jnp.sum(totals * lift, axis=0)
         lse_all[me, :HEADS, :] = top + jnp.log(total)
         lse_all[me, HEADS:, :] = (own_del[:HEADS, :] * own_lift + jnp.sum(parts * lift, axis=0)) / total
-        each_peer(lambda p: to_holder(lse_all, ls_s, ls_r, me, p).start())
+        to_holder(lse_all, ls_s, ls_r, me, FAR).start()
+
+        def both_sides(p):
+            to_holder(lse_all, ls_s, ls_r, me, FAR - p).start()
+            to_holder(lse_all, ls_s, ls_r, me, FAR + p).start()
+
+        loop(1, FAR, both_sides)
 
     def buffers(chain, D, d):
         return sb.at[chain, D, d - 1 - NEAR], rb.at[chain, D, d - 1 - NEAR]
@@ -364,6 +382,7 @@
             to_candidate(st_out, st_in, st_s, st_r, c, me).start()
 
     def gather_slot(s):
+        pace()
         query_step(s)
         grad_step(s - 1)
 
@@ -379,6 +398,7 @@
     bias_me = score_bias(me, 0)
     for h in range(HEADS):
         scores(me, 0, h, bias_me)
+    pace(False)
     query_step(1)
     gather_slot(2)
     loop(3, 7, gather_slot)
@@ -392,18 +412,20 @@
         own_weights_grad(h)
     dks[EMPTY] = jnp.zeros((BLK, DH), F32)
     dvs[EMPTY] = jnp.zeros((BLK, DH), F32)
+    pace()
     chain_step(0, 1)
     near_scores(0, 1)
     near_scores(1, 1)
-    for t in range(1, 9):
-        gather_sent(0, t)
+    pace()
     chain_step(0, 2)
     combine()
+    pace()
     chain_step(0, 3)
     near_scores(0, 2)
     near_scores(1, 2)
     for t in range(1, 9):
-        gather_sent(1, t)
+        gather_sent(0, t)
+    pace()
     chain_step(0, 4)
     each_peer(lambda p: to_holder(lse_all, ls_s, ls_r, wrap(me + p), p).wait_recv())
     fac[:, :HEADS, :] = jnp.exp(st_out[:, :HEADS, :] - lse_all[:, :HEADS, :])
@@ -411,26 +433,24 @@
     chain_grads(0)
     chain_step(1, 0)
     chain_grads(1)
+    pace()
     chain_step(0, 5)
     chain_step(1, 1)
     chain_grads(2)
     for D in range(2):
         grads(toward(D, 2), D, False)
+    own_grads()
+    pace()
     chain_step(1, 2)
     chain_grads(3)
     for D in range(2):
         grads(toward(D, 1), D, False)
+    near_grads(0, 1)
+    near_grads(1, 1)
+    pace()
     chain_step(1, 3)
     chain_grads(4)
-    own_grads()
-    near_grads(0, 1)
-    near_grads(1, 1)
-    chain_step(1, 4)
-    chain_grads(5)
-    chain_step(1, 5)
     grads(me, 0)
-    near_grads(0, 2)
-    near_grads(1, 2)
     last = NEAR + 1
     for h in range(HEADS):
         b, j = h // 2, h % 2
@@ -444,6 +464,15 @@
             r = came[b, MARK:, :].astype(F32)[8 * j : 8 * j + 1]
             x = x + came[b, head(j), :].astype(F32) * jnp.exp(r - lse_all[me, h : h + 1, :])
         att_ref[:, head(h)] = x.T.astype(BF16)
+    pace()
+    chain_step(1, 4)
+    chain_grads(5)
+    near_grads(0, 2)
+    near_grads(1, 2)
+    for t in range(1, 9):
+        gather_sent(1, t)
+    pace()
+    chain_step(1, 5)
     loop(0, CB_DEV, block_sum)
     each_peer(lambda p: to_candidate(st_out, st_in, st_s, st_r, wrap(me + p), me).wait_send())
     each_peer(lambda p: to_holder(lse_all, ls_s, ls_r, me, p).wait_send())
@@ -455,6 +484,8 @@
         chain_sent(0, i)
     for i in range(5):
         chain_sent(1, i)
+    if paired:
+        pl.semaphore_wait(pace_sem, 1)
     for h in range(HEADS):
         b, j = h // 2, h % 2
         x = own_qu[h] + qu[me, h]
@@ -499,6 +530,7 @@
             V((2 * NEAR,) + tile, F32), V((2 * NEAR, 8, 128), F32),
             D((2, 2, FAR, 2)), D((2, 2, FAR, 2)), D((2, 2, FAR, 2)), D((2, 2, FAR, 2)),
             D((N,)), D((N,)), D((N,)), D((N,)), D((2, NEAR, 2)), D((2, NEAR, 2)),
+            pltpu.SemaphoreType.REGULAR,
         ],
         compiler_params=pltpu.CompilerParams(
             collective_id=0, has_side_effects=True, vmem_limit_bytes=60 * 1024 * 1024

time: 141 us -> 138 us (0.979)
    pallas_call x1, Pallas kernels: 135 us -> 133 us  [ring(): pl.pallas_call(ring_kernel, in_specs=[pl.BlockSpec(memory_space=pltpu.SME...]
where the time goes in v7:
time: 138 us; the launch traced here: 136 us
  Pallas kernels  136 us (99%)
    pallas_call x1, Pallas kernels, ring(): pl.pallas_call(ring_kernel, in_specs=[pl.BlockSpec(memory_space=pltpu.SME...  133 us

profile of v7, /device:TPU:6, one launch (start us, length us, event | category | flops | bytes accessed | tf_op | source)
XLA Modules:
  0.0 136.3 jit_solution(7179337231043082284)
XLA Ops:
  0.6 133.2 %ring_attention.1 = (bf16[128,512]{1,0:T(8,128)(2,1)}, bf16[128,512]{1,0:T(8,128)(2,1)}, bf16[128,128]{1,0:T(8,128)(2,1)}, bf16[128,128]{1,0:T(8,128)(2,1)}, bf1...) custom-call(s32[16,24]{1,0:T(8,128)} %ids_ref.1, bf16[128,512]{1,0:T(8,128)(2,1)} %q_ref.1, ...), custom_call_target="tpu_custom_call" | custom-call | tf_op jit(solution)/shard_map/ring_attention/pallas_call | solution.py:507
  133.8 2.5 %hand_on.1 = (bf16[128,512]{1,0:T(8,128)(2,1)}, bf16[128,512]{1,0:T(8,128)(2,1)}, bf16[128,128]{1,0:T(8,128)(2,1)}, bf16[128,128]{1,0:T(8,128)(2,1)}, bf16[16,12...) custom-call(bf16[128,512]{1,0:T(8,128)(2,1)} %get-tuple-element.18.refs_0_, ...), custom_call_target="tpu_custom_call" | custom-call | tf_op jit(solution)/shard_map/hand_on/pallas_call | solution.py:550

commit v8 on v7

--- a/solution.py
+++ b/solution.py
@@ -253,6 +253,11 @@
             device_id={"ctx": toward(D, d)},
         )
 
+    def near_send(d):
+        for w in range(2):
+            for D in range(2):
+                near_copy(D, d, w).start()
+
     def near_scores(D, d):
         n = 2 * D + d - 1
         for w in range(2):
@@ -299,20 +304,24 @@
     def buffers(chain, D, d):
         return sb.at[chain, D, d - 1 - NEAR], rb.at[chain, D, d - 1 - NEAR]
 
-    def chain_copy(chain, D, d, b):
+    PARTS = (((0, 1), (2, 3)), ((0,), (1,), (2,), (3,)))
+
+    def chain_copy(chain, D, d, heads):
         src, dst = buffers(chain, D, d)
-        rows = pl.ds(0, MARK + 16 if chain == 0 else MARK)
+        b, j = heads[0] // 2, heads[0] % 2
+        rows = pl.ds(0, MARK + 16) if chain == 0 else pl.ds(j * 128, 128)
         return pltpu.make_async_remote_copy(
             src_ref=src.at[b, rows], dst_ref=dst.at[b, rows],
-            send_sem=c_send.at[chain, D, d - 1, b], recv_sem=c_recv.at[chain, D, d - 1, b],
+            send_sem=c_send.at[chain, D, d - 1, heads[0]], recv_sem=c_recv.at[chain, D, d - 1, heads[0]],
             device_id={"ctx": toward(D, NEAR + 1) if d == NEAR + 1 else nbr[D]},
         )
 
     def chain_step(chain, i):
         d = FAR - i
-        for b in range(2):
+        for heads in PARTS[chain]:
+            b = heads[0] // 2
             for D in ways(d + 1, b):
-                chain_copy(chain, D, d + 1, b).wait_recv()
+                chain_copy(chain, D, d + 1, heads).wait_recv()
             for D in ways(d, b):
                 c = toward(D, d)
                 out = buffers(chain, D, d)[0]
@@ -321,8 +330,8 @@
                 if chain == 0 and came:
                     old = arrived[b, MARK:, :].astype(F32)
                 marks = []
-                for j in range(2):
-                    h = 2 * b + j
+                for h in heads:
+                    j = h % 2
                     if chain == 0:
                         m = st_out[c, h : h + 1, :]
                         r = jnp.ceil(m * 0.25) * 4.0
@@ -340,12 +349,12 @@
                 if chain == 0:
                     out[b, MARK:, :] = jnp.concatenate(marks, axis=0).astype(out.dtype)
             for D in ways(d, b):
-                chain_copy(chain, D, d, b).start()
+                chain_copy(chain, D, d, heads).start()
 
     def chain_sent(chain, i):
-        for b in range(2):
-            for D in ways(FAR - i, b):
-                chain_copy(chain, D, FAR - i, b).wait_send()
+        for heads in PARTS[chain]:
+            for D in ways(FAR - i, heads[0] // 2):
+                chain_copy(chain, D, FAR - i, heads).wait_send()
 
     def chain_grads(i):
         if is_int(i) and i == 0:
@@ -391,8 +400,6 @@
     for d in range(1, NEAR + 1):
         for D in range(2):
             stage(toward(D, d))
-            for w in range(2):
-                near_copy(D, d, w).start()
     own_scores()
     stage(me)
     bias_me = score_bias(me, 0)
@@ -412,17 +419,17 @@
         own_weights_grad(h)
     dks[EMPTY] = jnp.zeros((BLK, DH), F32)
     dvs[EMPTY] = jnp.zeros((BLK, DH), F32)
+    near_send(1)
     pace()
     chain_step(0, 1)
+    near_send(2)
+    pace()
+    chain_step(0, 2)
+    combine()
+    pace()
+    chain_step(0, 3)
     near_scores(0, 1)
     near_scores(1, 1)
-    pace()
-    chain_step(0, 2)
-    combine()
-    pace()
-    chain_step(0, 3)
-    near_scores(0, 2)
-    near_scores(1, 2)
     for t in range(1, 9):
         gather_sent(0, t)
     pace()
@@ -443,10 +450,10 @@
     pace()
     chain_step(1, 2)
     chain_grads(3)
+    near_scores(0, 2)
+    near_scores(1, 2)
     for D in range(2):
         grads(toward(D, 1), D, False)
-    near_grads(0, 1)
-    near_grads(1, 1)
     pace()
     chain_step(1, 3)
     chain_grads(4)
@@ -459,7 +466,7 @@
             x = x + f_ou[n, h] * jnp.exp(f_max[n, h : h + 1, :] - lse_all[me, h : h + 1, :])
         for D in range(2):
             if j == 0:
-                chain_copy(0, D, last, b).wait_recv()
+                chain_copy(0, D, last, (h, h + 1)).wait_recv()
             came = buffers(0, D, last)[1]
             r = came[b, MARK:, :].astype(F32)[8 * j : 8 * j + 1]
             x = x + came[b, head(j), :].astype(F32) * jnp.exp(r - lse_all[me, h : h + 1, :])
@@ -467,6 +474,8 @@
     pace()
     chain_step(1, 4)
     chain_grads(5)
+    near_grads(0, 1)
+    near_grads(1, 1)
     near_grads(0, 2)
     near_grads(1, 2)
     for t in range(1, 9):
@@ -490,8 +499,7 @@
         b, j = h // 2, h % 2
         x = own_qu[h] + qu[me, h]
         for D in range(2):
-            if j == 0:
-                chain_copy(1, D, last, b).wait_recv()
+            chain_copy(1, D, last, (h,)).wait_recv()
             x = x + buffers(1, D, last)[1][b, head(j), :].astype(F32)
         qg_ref[:, head(h)] = (x * SCALE).T.astype(BF16)
     chain_sent(1, 5)
@@ -528,7 +536,7 @@
             V((2 * NEAR, KEYS, DH), BF16), V((2 * NEAR, KEYS, DH), BF16),
             V((2 * NEAR, HEADS, KEYS, 128), F32), V((2 * NEAR, HEADS, KEYS, 128), F32),
             V((2 * NEAR,) + tile, F32), V((2 * NEAR, 8, 128), F32),
-            D((2, 2, FAR, 2)), D((2, 2, FAR, 2)), D((2, 2, FAR, 2)), D((2, 2, FAR, 2)),
+            D((2, 2, FAR, 2)), D((2, 2, FAR, 2)), D((2, 2, FAR, HEADS)), D((2, 2, FAR, HEADS)),
             D((N,)), D((N,)), D((N,)), D((N,)), D((2, NEAR, 2)), D((2, NEAR, 2)),
             pltpu.SemaphoreType.REGULAR,
         ],

time: 138 us -> 137 us (level); the launches traced: 136 us -> 137 us
  no operation moved by 1% of the time
where the time goes in v8:
time: 137 us
  Pallas kernels  136 us (99%)
    pallas_call x1, Pallas kernels, ring(): pl.pallas_call(ring_kernel, in_specs=[pl.BlockSpec(memory_space=pltpu.SME...  134 us

profile of v8, /device:TPU:6, one launch (start us, length us, event | category | flops | bytes accessed | tf_op | source)
XLA Modules:
  0.0 136.7 jit_solution(377005080257974997)
XLA Ops:
  0.6 133.6 %ring_attention.1 = (bf16[128,512]{1,0:T(8,128)(2,1)}, bf16[128,512]{1,0:T(8,128)(2,1)}, bf16[128,128]{1,0:T(8,128)(2,1)}, bf16[128,128]{1,0:T(8,128)(2,1)}, bf1...) custom-call(s32[16,24]{1,0:T(8,128)} %ids_ref.1, bf16[128,512]{1,0:T(8,128)(2,1)} %q_ref.1, ...), custom_call_target="tpu_custom_call" | custom-call | tf_op jit(solution)/shard_map/ring_attention/pallas_call | solution.py:515
  134.2 2.5 %hand_on.1 = (bf16[128,512]{1,0:T(8,128)(2,1)}, bf16[128,512]{1,0:T(8,128)(2,1)}, bf16[128,128]{1,0:T(8,128)(2,1)}, bf16[128,128]{1,0:T(8,128)(2,1)}, bf16[16,12...) custom-call(bf16[128,512]{1,0:T(8,128)(2,1)} %get-tuple-element.18.refs_0_, ...), custom_call_target="tpu_custom_call" | custom-call | tf_op jit(solution)/shard_map/hand_on/pallas_call | solution.py:558

commit v9 on v8

--- a/solution.py
+++ b/solution.py
@@ -45,19 +45,25 @@
 
 
 def ring_kernel(
-    ids_ref, q_ref, k_ref, v_ref, ok_ref, ov_ref, g_ref,
+    ids_ref, q_ref, k_hbm, v_hbm, ok_ref, ov_ref, g_ref,
     att_ref, qg_ref, okg_ref, ovg_ref, dk_ref, dv_ref,
     q_all, g_all, nk, nv, lw, dp, ou, qu,
     own_lw, own_dp, own_ou, own_qu, own_st, own_del,
     st_out, st_in, lse_all, fac,
     ds_t, p_t, tr, dks, dvs, sel, sb, rb,
     fk, fv, f_lw, f_dp, f_ou, f_max,
-    g_send, g_recv, c_send, c_recv, st_s, st_r, ls_s, ls_r, f_send, f_recv, pace_sem,
+    g_send, g_recv, c_send, c_recv, st_s, st_r, ls_s, ls_r, f_send, f_recv, pace_sem, k_ref, v_ref, kv_sem,
 ):
     me = lax.axis_index("ctx")
     low = me * CB_DEV
     nbr = (wrap(me + 1), wrap(me - 1))
 
+    blocks_in = (
+        pltpu.make_async_copy(k_hbm, k_ref, kv_sem.at[0]),
+        pltpu.make_async_copy(v_hbm, v_ref, kv_sem.at[1]),
+    )
+    for copy in blocks_in:
+        copy.start()
     barrier = pltpu.get_barrier_semaphore()
 
     def loop(lo, hi, fn):
@@ -74,11 +80,10 @@
     side = lax.axis_index("head")
     other = side + 1 - 2 * lax.rem(side, 2)
 
-    def pace(wait=True):
+    def pace():
         if paired:
             pl.semaphore_signal(pace_sem, inc=1, device_id={"head": other})
-            if wait:
-                pl.semaphore_wait(pace_sem, 1)
+            pl.semaphore_wait(pace_sem, 1)
 
     each_peer(lambda p: pl.semaphore_signal(barrier, inc=1, device_id={"ctx": wrap(me + p)}))
     if paired:
@@ -397,6 +402,8 @@
 
     gather_first(0)
     gather_first(1)
+    for copy in blocks_in:
+        copy.wait()
     for d in range(1, NEAR + 1):
         for D in range(2):
             stage(toward(D, d))
@@ -405,7 +412,7 @@
     bias_me = score_bias(me, 0)
     for h in range(HEADS):
         scores(me, 0, h, bias_me)
-    pace(False)
+    pace()
     query_step(1)
     gather_slot(2)
     loop(3, 7, gather_slot)
@@ -434,6 +441,8 @@
         gather_sent(0, t)
     pace()
     chain_step(0, 4)
+    near_scores(0, 2)
+    near_scores(1, 2)
     each_peer(lambda p: to_holder(lse_all, ls_s, ls_r, wrap(me + p), p).wait_recv())
     fac[:, :HEADS, :] = jnp.exp(st_out[:, :HEADS, :] - lse_all[:, :HEADS, :])
 
@@ -450,8 +459,6 @@
     pace()
     chain_step(1, 2)
     chain_grads(3)
-    near_scores(0, 2)
-    near_scores(1, 2)
     for D in range(2):
         grads(toward(D, 1), D, False)
     pace()
@@ -493,8 +500,6 @@
         chain_sent(0, i)
     for i in range(5):
         chain_sent(1, i)
-    if paired:
-        pl.semaphore_wait(pace_sem, 1)
     for h in range(HEADS):
         b, j = h // 2, h % 2
         x = own_qu[h] + qu[me, h]
@@ -507,6 +512,7 @@
 
 def ring(ids, q, k, v, ok, ov, g):
     vm = pl.BlockSpec(memory_space=pltpu.VMEM)
+    hbm = pl.BlockSpec(memory_space=pl.ANY)
     shape = jax.ShapeDtypeStruct
     V = pltpu.VMEM
     D = pltpu.SemaphoreType.DMA
@@ -514,7 +520,7 @@
     tile = (HEADS, 128, 128)
     return pl.pallas_call(
         ring_kernel,
-        in_specs=[pl.BlockSpec(memory_space=pltpu.SMEM)] + [vm] * 6,
+        in_specs=[pl.BlockSpec(memory_space=pltpu.SMEM), vm, hbm, hbm, vm, vm, vm],
         out_specs=[vm] * 6,
         out_shape=[
             shape((128, ROWS), BF16), shape((128, ROWS), BF16),
@@ -539,6 +545,7 @@
             D((2, 2, FAR, 2)), D((2, 2, FAR, 2)), D((2, 2, FAR, HEADS)), D((2, 2, FAR, HEADS)),
             D((N,)), D((N,)), D((N,)), D((N,)), D((2, NEAR, 2)), D((2, NEAR, 2)),
             pltpu.SemaphoreType.REGULAR,
+            V((CB_DEV, BLK, DH), BF16), V((CB_DEV, BLK, DH), BF16), D((2,)),
         ],
         compiler_params=pltpu.CompilerParams(
             collective_id=0, has_side_effects=True, vmem_limit_bytes=60 * 1024 * 1024
@@ -548,18 +555,29 @@
 
 
 def hand_on_kernel(*refs):
-    n = len(refs) // 2
+    n = (len(refs) - 2) // 3
+    held = refs[2 * n : 3 * n]
+    into = [pltpu.make_async_copy(refs[j], held[j], refs[3 * n].at[j]) for j in range(n)]
+    out = [pltpu.make_async_copy(held[j], refs[n + j], refs[3 * n + 1].at[j]) for j in range(n)]
+    for copy in into:
+        copy.start()
     for j in range(n):
-        refs[n + j][...] = refs[j][...]
+        into[j].wait()
+        out[j].start()
+    for copy in out:
+        copy.wait()
 
 
 def hand_on(parts):
-    vm = pl.BlockSpec(memory_space=pltpu.VMEM)
+    hbm = pl.BlockSpec(memory_space=pl.ANY)
+    n = len(parts)
     return pl.pallas_call(
         hand_on_kernel,
-        in_specs=[vm] * len(parts),
-        out_specs=[vm] * len(parts),
+        in_specs=[hbm] * n,
+        out_specs=[hbm] * n,
         out_shape=[jax.ShapeDtypeStruct(x.shape, x.dtype) for x in parts],
+        scratch_shapes=[pltpu.VMEM(x.shape, x.dtype) for x in parts]
+        + [pltpu.SemaphoreType.DMA((n,)), pltpu.SemaphoreType.DMA((n,))],
         compiler_params=pltpu.CompilerParams(vmem_limit_bytes=60 * 1024 * 1024),
         name="hand_on",
     )(*parts)

time: 137 us -> 140 us (1.022)
  Pallas kernels: 136 us -> 139 us
    pallas_call x1, Pallas kernels: 134 us -> 137 us  [ring(): pl.pallas_call(ring_kernel, in_specs=[pl.BlockSpec(memory_space=pltpu.SME...]
where the time goes in v9:
time: 140 us
  Pallas kernels  139 us (99%)
    pallas_call x1, Pallas kernels, ring(): pl.pallas_call(ring_kernel, in_specs=[pl.BlockSpec(memory_space=pltpu.SME...  137 us

profile of v9, /device:TPU:6, one launch (start us, length us, event | category | flops | bytes accessed | tf_op | source)
XLA Modules:
  0.0 139.9 jit_solution(5434287905444169780)
XLA Ops:
  0.6 136.8 %ring_attention.1 = (bf16[128,512]{1,0:T(8,128)(2,1)}, bf16[128,512]{1,0:T(8,128)(2,1)}, bf16[128,128]{1,0:T(8,128)(2,1)}, bf16[128,128]{1,0:T(8,128)(2,1)}, bf1...) custom-call(s32[16,24]{1,0:T(8,128)} %ids_ref.1, bf16[128,512]{1,0:T(8,128)(2,1)} %q_ref.1, ...), custom_call_target="tpu_custom_call" | custom-call | tf_op jit(solution)/shard_map/ring_attention/pallas_call | solution.py:521
  137.5 2.3 %hand_on.1 = (bf16[128,512]{1,0:T(8,128)(2,1)}, bf16[128,512]{1,0:T(8,128)(2,1)}, bf16[128,128]{1,0:T(8,128)(2,1)}, bf16[128,128]{1,0:T(8,128)(2,1)}, bf16[16,12...) custom-call(bf16[128,512]{1,0:T(8,128)(2,1)} %get-tuple-element.18.refs_0_, ...), custom_call_target="tpu_custom_call" | custom-call | tf_op jit(solution)/shard_map/hand_on/pallas_call | solution.py:574

commit v10 on v9

--- a/solution.py
+++ b/solution.py
@@ -80,10 +80,11 @@
     side = lax.axis_index("head")
     other = side + 1 - 2 * lax.rem(side, 2)
 
-    def pace():
+    def pace(wait=True):
         if paired:
             pl.semaphore_signal(pace_sem, inc=1, device_id={"head": other})
-            pl.semaphore_wait(pace_sem, 1)
+            if wait:
+                pl.semaphore_wait(pace_sem, 1)
 
     each_peer(lambda p: pl.semaphore_signal(barrier, inc=1, device_id={"ctx": wrap(me + p)}))
     if paired:
@@ -412,7 +413,7 @@
     bias_me = score_bias(me, 0)
     for h in range(HEADS):
         scores(me, 0, h, bias_me)
-    pace()
+    pace(False)
     query_step(1)
     gather_slot(2)
     loop(3, 7, gather_slot)
@@ -500,6 +501,8 @@
         chain_sent(0, i)
     for i in range(5):
         chain_sent(1, i)
+    if paired:
+        pl.semaphore_wait(pace_sem, 1)
     for h in range(HEADS):
         b, j = h // 2, h % 2
         x = own_qu[h] + qu[me, h]

time: 140 us -> 136 us (0.971)
  Pallas kernels: 139 us -> 135 us
    pallas_call x1, Pallas kernels: 137 us -> 133 us  [ring(): pl.pallas_call(ring_kernel, in_specs=[pl.BlockSpec(memory_space=pltpu.SME...]
where the time goes in v10:
time: 136 us
  Pallas kernels  135 us (99%)
    pallas_call x1, Pallas kernels, ring(): pl.pallas_call(ring_kernel, in_specs=[pl.BlockSpec(memory_space=pltpu.SME...  133 us

profile of v10, /device:TPU:6, one launch (start us, length us, event | category | flops | bytes accessed | tf_op | source)
XLA Modules:
  0.0 135.7 jit_solution(18068755191694928137)
XLA Ops:
  0.6 132.6 %ring_attention.1 = (bf16[128,512]{1,0:T(8,128)(2,1)}, bf16[128,512]{1,0:T(8,128)(2,1)}, bf16[128,128]{1,0:T(8,128)(2,1)}, bf16[128,128]{1,0:T(8,128)(2,1)}, bf1...) custom-call(s32[16,24]{1,0:T(8,128)} %ids_ref.1, bf16[128,512]{1,0:T(8,128)(2,1)} %q_ref.1, ...), custom_call_target="tpu_custom_call" | custom-call | tf_op jit(solution)/shard_map/ring_attention/pallas_call | solution.py:524
  133.2 2.3 %hand_on.1 = (bf16[128,512]{1,0:T(8,128)(2,1)}, bf16[128,512]{1,0:T(8,128)(2,1)}, bf16[128,128]{1,0:T(8,128)(2,1)}, bf16[128,128]{1,0:T(8,128)(2,1)}, bf16[16,12...) custom-call(bf16[128,512]{1,0:T(8,128)(2,1)} %get-tuple-element.18.refs_0_, ...), custom_call_target="tpu_custom_call" | custom-call | tf_op jit(solution)/shard_map/hand_on/pallas_call | solution.py:577

commit v11 on v10

--- a/solution.py
+++ b/solution.py
@@ -440,10 +440,6 @@
     near_scores(1, 1)
     for t in range(1, 9):
         gather_sent(0, t)
-    pace()
-    chain_step(0, 4)
-    near_scores(0, 2)
-    near_scores(1, 2)
     each_peer(lambda p: to_holder(lse_all, ls_s, ls_r, wrap(me + p), p).wait_recv())
     fac[:, :HEADS, :] = jnp.exp(st_out[:, :HEADS, :] - lse_all[:, :HEADS, :])
 
@@ -451,13 +447,16 @@
     chain_step(1, 0)
     chain_grads(1)
     pace()
-    chain_step(0, 5)
+    chain_step(0, 4)
     chain_step(1, 1)
     chain_grads(2)
+    near_scores(0, 2)
+    near_scores(1, 2)
     for D in range(2):
         grads(toward(D, 2), D, False)
     own_grads()
     pace()
+    chain_step(0, 5)
     chain_step(1, 2)
     chain_grads(3)
     for D in range(2):

time: 136 us -> 135 us (level)
  Pallas kernels: 135 us -> 133 us
    pallas_call x1, Pallas kernels: 133 us -> 131 us  [ring(): pl.pallas_call(ring_kernel, in_specs=[pl.BlockSpec(memory_space=pltpu.SME...]
where the time goes in v11:
time: 135 us; the launch traced here: 134 us
  Pallas kernels  133 us (99%)
    pallas_call x1, Pallas kernels, ring(): pl.pallas_call(ring_kernel, in_specs=[pl.BlockSpec(memory_space=pltpu.SME...  131 us

profile of v11, /device:TPU:6, one launch (start us, length us, event | category | flops | bytes accessed | tf_op | source)
XLA Modules:
  0.0 134.3 jit_solution(11997887238141079116)
XLA Ops:
  0.6 131.2 %ring_attention.1 = (bf16[128,512]{1,0:T(8,128)(2,1)}, bf16[128,512]{1,0:T(8,128)(2,1)}, bf16[128,128]{1,0:T(8,128)(2,1)}, bf16[128,128]{1,0:T(8,128)(2,1)}, bf1...) custom-call(s32[16,24]{1,0:T(8,128)} %ids_ref.1, bf16[128,512]{1,0:T(8,128)(2,1)} %q_ref.1, ...), custom_call_target="tpu_custom_call" | custom-call | tf_op jit(solution)/shard_map/ring_attention/pallas_call | solution.py:523
  131.8 2.3 %hand_on.1 = (bf16[128,512]{1,0:T(8,128)(2,1)}, bf16[128,512]{1,0:T(8,128)(2,1)}, bf16[128,128]{1,0:T(8,128)(2,1)}, bf16[128,128]{1,0:T(8,128)(2,1)}, bf16[16,12...) custom-call(bf16[128,512]{1,0:T(8,128)(2,1)} %get-tuple-element.18.refs_0_, ...), custom_call_target="tpu_custom_call" | custom-call | tf_op jit(solution)/shard_map/hand_on/pallas_call | solution.py:576
